TPU v7x, 32 devices: a whole 2x2x4 slice. The times are simulated.
32 devices in a mesh: dp: 2 (over core), fsdp: 16 (over z, y, x).
Axes of the slice: x: 2, y: 2, z: 4, core: 2. Of those that a mesh axis runs over, the one named last changes fastest.
Arguments:
- tokens: bfloat16 [2, 8192, 768], P(None, ('dp', 'fsdp')), may hold values from -6 to 6
- cotangent: bfloat16 [2, 8192, 768], P(None, ('dp', 'fsdp')), may hold values from -6 to 6
- routes: int32 [2, 8192, 1], P(None, ('dp', 'fsdp')), may hold values from 0 to 15
- lengths: int32 [2, 32, 2], P(None, ('dp', 'fsdp')), may hold values from 32 to 224, as said below
- norm1_gain: bfloat16 [768], P(('dp', 'fsdp')), may hold values from 0.5 to 1.5
- input_weight: bfloat16 [768, 3072], P(('dp', 'fsdp')), may hold values from -0.21875 to 0.21875
- conv_weight: bfloat16 [1536, 4], P(('dp', 'fsdp')), may hold values from -3 to 3
- conv_bias: bfloat16 [1536], P(('dp', 'fsdp')), may hold values from -1.5 to 1.5
- scan_weight: bfloat16 [1536, 80], P(('dp', 'fsdp')), may hold values from -0.15625 to 0.15625
- step_weight: bfloat16 [1536, 48], P(('dp', 'fsdp')), may hold values from -0.875 to 0.875
- step_bias: bfloat16 [1536], P(('dp', 'fsdp')), may hold values from -4.59375 to -2.296875
- decay_log: bfloat16 [1536, 16], P(('dp', 'fsdp')), may hold values from 0 to 2.765625
- skip_gain: bfloat16 [1536], P(('dp', 'fsdp')), may hold values from 0.5 to 1.5
- out_weight: bfloat16 [1536, 768], P(('dp', 'fsdp')), may hold values from -0.15625 to 0.15625
- norm2_gain: bfloat16 [768], P(('dp', 'fsdp')), may hold values from 0.5 to 1.5
- router_weight: bfloat16 [768, 16], P(('dp', 'fsdp')), may hold values from -0.15625 to 0.15625
- expert_up: bfloat16 [16, 768, 3072], P('fsdp', None, 'dp'), may hold values from -0.21875 to 0.21875
- expert_down: bfloat16 [16, 3072, 768], P('fsdp', 'dp'), may hold values from -1.75 to 1.75
Outputs:
- block_output: bfloat16 [2, 8192, 768], P(None, ('dp', 'fsdp'))
- tokens_grad: float32 [2, 8192, 768], P(None, ('dp', 'fsdp'))
- norm1_gain_grad: float32 [768], P(('dp', 'fsdp'))
- input_weight_grad: float32 [768, 3072], P(('dp', 'fsdp'))
- conv_weight_grad: float32 [1536, 4], P(('dp', 'fsdp'))
- conv_bias_grad: float32 [1536], P(('dp', 'fsdp'))
- scan_weight_grad: float32 [1536, 80], P(('dp', 'fsdp'))
- step_weight_grad: float32 [1536, 48], P(('dp', 'fsdp'))
- step_bias_grad: float32 [1536], P(('dp', 'fsdp'))
- decay_log_grad: float32 [1536, 16], P(('dp', 'fsdp'))
- skip_gain_grad: float32 [1536], P(('dp', 'fsdp'))
- out_weight_grad: float32 [1536, 768], P(('dp', 'fsdp'))
- norm2_gain_grad: float32 [768], P(('dp', 'fsdp'))
- router_weight_grad: float32 [768, 16], P(('dp', 'fsdp'))
- expert_up_grad: float32 [16, 768, 3072], P('fsdp', None, 'dp')
- expert_down_grad: float32 [16, 3072, 768], P('fsdp', 'dp')
Inputs may be any that keep to these rules, and one draw needn't show every extreme that they name: `routes`: routes of padding rows are ignored. `lengths`: A pack's two entries sum to 256: first its sample's length, from 128 to 224, then its padding. In every micro-batch some pack has the longest sample and another the shortest.
All inputs are finite; a program needn't handle non-finite values.
Results may differ from a plain program's by a relative error of at most 0.013.
Values may be sent and summed in bfloat16 or wider, within the bound.
No kernel may reach another device: no remote copies, remote signals or barrier semaphores. Data moves between devices by JAX's collectives and lax.ppermute only.
A program may use at most 256 MiB of HBM per device.

v0:
```python
import jax
import jax.numpy as jnp
from jax import lax
from jax.sharding import PartitionSpec as P

EPSILON = 1e-05


def segment_rows(lengths_row, steps):
    ends = jnp.cumsum(lengths_row)
    places = jnp.arange(steps, dtype=jnp.int32)
    segment = jnp.sum((places[:, None] >= ends[None, :]).astype(jnp.int32), axis=1)
    previous = jnp.concatenate([jnp.full((1,), -1, jnp.int32), segment[:-1]])
    live = (segment < lengths_row.shape[0] - 1).astype(jnp.int32)
    carried = (segment == previous).astype(jnp.float32)
    return (segment, live, carried)


def conv_silu(branch_x, segment, conv_weight, conv_bias):
    kernel = conv_weight.shape[1]
    width = branch_x.shape[1]
    total = conv_bias[None, :] + conv_weight[:, kernel - 1][None, :] * branch_x
    for shift in range(1, kernel):
        moved = jnp.concatenate([jnp.zeros((shift, width), jnp.float32), branch_x[:-shift]], axis=0)
        moved_segment = jnp.concatenate([jnp.full((shift,), -1, jnp.int32), segment[:-shift]])
        same = (moved_segment == segment).astype(jnp.float32)
        total = total + conv_weight[:, kernel - 1 - shift][None, :] * moved * same[:, None]
    return jax.nn.silu(total)


def scan_blocks(scan_in, step_size, bmat, cmat, decay_mat, carried):
    steps, width = scan_in.shape
    states = decay_mat.shape[0]
    span = min(32, steps)
    count = steps // span

    def one_step(state, item):
        size_t, input_t, bvec, cvec, carry_t = item
        state = (
            jnp.exp(size_t[None, :] * decay_mat) * carry_t * state
            + bvec[:, None] * (size_t * input_t)[None, :]
        )
        return (state, jnp.sum(cvec[:, None] * state, axis=0))

    @jax.checkpoint
    def block_step(state, block):
        return lax.scan(one_step, state, block, unroll=8)

    blocks = (
        step_size.reshape(count, span, width),
        scan_in.reshape(count, span, width),
        bmat.reshape(count, span, states),
        cmat.reshape(count, span, states),
        carried.reshape(count, span),
    )
    final, outputs = lax.scan(block_step, jnp.zeros((states, width), jnp.float32), blocks)
    return outputs.reshape(steps, width)


def to_experts(values):
    return lax.all_to_all(values, "fsdp", split_axis=0, concat_axis=0, tiled=True)


def from_experts(values):
    return lax.all_to_all(values, "fsdp", split_axis=0, concat_axis=0, tiled=True)


def norm_backward(grad_normed, gain, normed, inv_scale):
    scaled = grad_normed * gain
    grad_in = inv_scale * (scaled - normed * jnp.mean(scaled * normed, axis=-1, keepdims=True))
    return (grad_in, jnp.sum(grad_normed * normed, axis=0))


def body(
    tokens,
    cotangent,
    routes,
    lengths,
    norm1_gain,
    input_weight,
    conv_weight,
    conv_bias,
    scan_weight,
    step_weight,
    step_bias,
    decay_log,
    skip_gain,
    out_weight,
    norm2_gain,
    router_weight,
    expert_up,
    expert_down,
):
    micro = tokens.shape[0]
    steps = tokens.shape[1]
    model = tokens.shape[2]
    experts = lax.axis_size("fsdp")
    capacity = (5 * steps + 4 * experts - 1) // (4 * experts)
    shards = (
        norm1_gain,
        input_weight,
        conv_weight,
        conv_bias,
        scan_weight,
        step_weight,
        step_bias,
        decay_log,
        skip_gain,
        out_weight,
        norm2_gain,
        router_weight,
    )
    mamba_acc = tuple((jnp.zeros(piece.shape, jnp.float32) for piece in shards))
    up_acc = jnp.zeros(
        (1, expert_up.shape[1], expert_up.shape[2] * lax.axis_size("dp")), jnp.float32
    )
    down_acc = jnp.zeros(
        (1, expert_down.shape[1] * lax.axis_size("dp"), expert_down.shape[2]), jnp.float32
    )
    slot_ids = jnp.arange(experts * capacity, dtype=jnp.int32)
    expert_ids = jnp.arange(experts, dtype=jnp.int32)
    outputs = []
    input_grads = []
    for index in range(micro):
        gathered = (
            lax.all_gather(norm1_gain, ("dp", "fsdp"), axis=0, tiled=True),
            lax.all_gather(input_weight, ("dp", "fsdp"), axis=0, tiled=True),
            lax.all_gather(conv_weight, ("dp", "fsdp"), axis=0, tiled=True),
            lax.all_gather(conv_bias, ("dp", "fsdp"), axis=0, tiled=True),
            lax.all_gather(scan_weight, ("dp", "fsdp"), axis=0, tiled=True),
            lax.all_gather(step_weight, ("dp", "fsdp"), axis=0, tiled=True),
            lax.all_gather(step_bias, ("dp", "fsdp"), axis=0, tiled=True),
            lax.all_gather(decay_log, ("dp", "fsdp"), axis=0, tiled=True),
            lax.all_gather(skip_gain, ("dp", "fsdp"), axis=0, tiled=True),
            lax.all_gather(out_weight, ("dp", "fsdp"), axis=0, tiled=True),
            lax.all_gather(norm2_gain, ("dp", "fsdp"), axis=0, tiled=True),
            lax.all_gather(router_weight, ("dp", "fsdp"), axis=0, tiled=True),
        )
        (
            gain_first,
            input_full,
            kernel_full,
            bias_conv,
            select_full,
            step_full,
            bias_step,
            decay_full,
            skip_full,
            output_full,
            gain_second,
            router_full,
        ) = gathered
        up_full, down_full = (
            lax.all_gather(expert_up, "dp", axis=2, tiled=True),
            lax.all_gather(expert_down, "dp", axis=1, tiled=True),
        )
        up_use = up_full[0]
        down_use = down_full[0]
        hidden = tokens[index].astype(jnp.float32)
        segment, live, carried = segment_rows(lengths[index, 0], steps)
        live_float = live.astype(jnp.float32)
        gain_one = gain_first.astype(jnp.float32)
        inv_first = lax.rsqrt(jnp.mean(hidden * hidden, axis=-1, keepdims=True) + EPSILON)
        normed_first = hidden * inv_first
        normed_low = (normed_first * gain_one).astype(jnp.bfloat16)
        projected = jnp.dot(normed_low, input_full, preferred_element_type=jnp.float32)
        inner = projected.shape[1] // 2
        branch_x = projected[:, :inner]
        branch_z = projected[:, inner:]

        def conv_piece(values, kernel_values, bias_values):
            return conv_silu(values, segment, kernel_values, bias_values)

        scan_in, conv_pull = jax.vjp(
            conv_piece, branch_x, kernel_full.astype(jnp.float32), bias_conv.astype(jnp.float32)
        )
        scan_low = scan_in.astype(jnp.bfloat16)
        selected = jnp.dot(scan_low, select_full, preferred_element_type=jnp.float32)
        rank = step_full.shape[1]
        states = decay_full.shape[1]
        rank_low = selected[:, :rank].astype(jnp.bfloat16)
        bmat = selected[:, rank : rank + states]
        cmat = selected[:, rank + states :]
        step_pre = jnp.einsum(
            "tr,cr->tc", rank_low, step_full, preferred_element_type=jnp.float32
        ) + bias_step.astype(jnp.float32)
        step_size = jax.nn.softplus(step_pre)
        decay_mat = (-jnp.exp(decay_full.astype(jnp.float32))).T

        def scan_piece(values, sizes, bvalues, cvalues, decays):
            return scan_blocks(values, sizes, bvalues, cvalues, decays, carried)

        scanned, scan_pull = jax.vjp(scan_piece, scan_in, step_size, bmat, cmat, decay_mat)
        skip_one = skip_full.astype(jnp.float32)
        mixer_out = scanned + skip_one * scan_in
        sigmoid_z = jax.nn.sigmoid(branch_z)
        silu_z = branch_z * sigmoid_z
        gated_low = (mixer_out * silu_z).astype(jnp.bfloat16)
        mixed = jnp.dot(gated_low, output_full, preferred_element_type=jnp.float32)
        residual = hidden + live_float[:, None] * mixed
        gain_two = gain_second.astype(jnp.float32)
        inv_second = lax.rsqrt(jnp.mean(residual * residual, axis=-1, keepdims=True) + EPSILON)
        normed_second = residual * inv_second
        routed = (normed_second * gain_two).astype(jnp.bfloat16)
        logits = jnp.dot(routed, router_full, preferred_element_type=jnp.float32)
        probs = jax.nn.softmax(logits, axis=-1)
        route = routes[index, :, 0]
        route_hot = (route[:, None] == expert_ids[None, :]).astype(jnp.int32)
        live_hot = route_hot * live[:, None]
        before = jnp.cumsum(live_hot, axis=0) - live_hot
        slot = jnp.sum(before * live_hot, axis=1)
        kept = live * (slot < capacity).astype(jnp.int32)
        route_float = route_hot.astype(jnp.float32)
        gate = jnp.sum(probs * route_float, axis=1)
        weight_row = gate * kept.astype(jnp.float32)
        target = route * capacity + slot
        chooser = ((slot_ids[:, None] == target[None, :]) & (kept[None, :] == 1)).astype(
            jnp.bfloat16
        )
        send = (
            jnp.dot(chooser, routed, preferred_element_type=jnp.float32)
            .astype(jnp.bfloat16)
            .reshape(experts, capacity, model)
        )
        received = to_experts(send)
        flat_in = received.reshape(-1, model)
        pre = jnp.dot(flat_in, up_use, preferred_element_type=jnp.float32)
        act, gelu_pull = jax.vjp(jax.nn.gelu, pre)
        act_low = act.astype(jnp.bfloat16)
        expert_out = jnp.dot(act_low, down_use, preferred_element_type=jnp.float32).reshape(
            received.shape
        )
        result = expert_out.astype(jnp.bfloat16)
        returned = from_experts(result)
        back = jnp.einsum(
            "st,sd->td", chooser, returned.reshape(-1, model), preferred_element_type=jnp.float32
        )
        outputs.append((residual + weight_row[:, None] * back).astype(jnp.bfloat16))
        upstream = cotangent[index].astype(jnp.float32)
        grad_result = (weight_row[:, None] * upstream).astype(jnp.bfloat16)
        grad_gate = kept.astype(jnp.float32) * jnp.sum(upstream * back, axis=1)
        grad_logits = ((grad_gate * gate)[:, None] * (route_float - probs)).astype(jnp.bfloat16)
        router_grad = jnp.einsum(
            "td,te->de", routed, grad_logits, preferred_element_type=jnp.float32
        )
        grad_routed = jnp.einsum(
            "te,de->td", grad_logits, router_full, preferred_element_type=jnp.float32
        )
        grad_send = (
            jnp.dot(chooser, grad_result, preferred_element_type=jnp.float32)
            .astype(jnp.bfloat16)
            .reshape(experts, capacity, model)
        )
        grad_received = to_experts(grad_send)
        flat_grad = grad_received.reshape(-1, model)
        grad_act = jnp.einsum("rd,fd->rf", flat_grad, down_use, preferred_element_type=jnp.float32)
        grad_pre = gelu_pull(grad_act)[0].astype(jnp.bfloat16)
        down_acc = (
            down_acc
            + jnp.einsum("rf,rd->fd", act_low, flat_grad, preferred_element_type=jnp.float32)[None]
        )
        up_acc = (
            up_acc
            + jnp.einsum("rd,rf->df", flat_in, grad_pre, preferred_element_type=jnp.float32)[None]
        )
        grad_rows = jnp.einsum(
            "rf,df->rd", grad_pre, up_use, preferred_element_type=jnp.float32
        ).reshape(grad_received.shape)
        grad_back = grad_rows.astype(jnp.bfloat16)
        grad_returned = from_experts(grad_back)
        grad_routed = grad_routed + jnp.einsum(
            "st,sd->td",
            chooser,
            grad_returned.reshape(-1, model),
            preferred_element_type=jnp.float32,
        )
        grad_norm_two, gain_two_grad = norm_backward(
            grad_routed, gain_two, normed_second, inv_second
        )
        grad_residual = upstream + grad_norm_two
        grad_mixed = (live_float[:, None] * grad_residual).astype(jnp.bfloat16)
        output_grad = jnp.einsum(
            "tc,td->cd", gated_low, grad_mixed, preferred_element_type=jnp.float32
        )
        grad_gated = jnp.einsum(
            "td,cd->tc", grad_mixed, output_full, preferred_element_type=jnp.float32
        )
        grad_mixer = grad_gated * silu_z
        grad_branch_z = grad_gated * mixer_out * sigmoid_z * (1.0 + branch_z * (1.0 - sigmoid_z))
        grad_scan_in, grad_step, grad_bmat, grad_cmat, grad_decay = scan_pull(grad_mixer)
        skip_grad = jnp.sum(grad_mixer * scan_in, axis=0)
        decay_grad = (grad_decay * decay_mat).T
        grad_step_pre = grad_step * jax.nn.sigmoid(step_pre)
        step_bias_grad = jnp.sum(grad_step_pre, axis=0)
        grad_step_low = grad_step_pre.astype(jnp.bfloat16)
        step_grad = jnp.einsum(
            "tc,tr->cr", grad_step_low, rank_low, preferred_element_type=jnp.float32
        )
        grad_rank = jnp.einsum(
            "tc,cr->tr", grad_step_low, step_full, preferred_element_type=jnp.float32
        )
        grad_selected = jnp.concatenate([grad_rank, grad_bmat, grad_cmat], axis=1).astype(
            jnp.bfloat16
        )
        select_grad = jnp.einsum(
            "tc,tk->ck", scan_low, grad_selected, preferred_element_type=jnp.float32
        )
        grad_values = jnp.einsum(
            "tk,ck->tc", grad_selected, select_full, preferred_element_type=jnp.float32
        )
        grad_conv_out = grad_values + grad_scan_in + grad_mixer * skip_one
        grad_branch_x, kernel_grad, conv_bias_grad = conv_pull(grad_conv_out)
        grad_projected = jnp.concatenate([grad_branch_x, grad_branch_z], axis=1).astype(
            jnp.bfloat16
        )
        input_grad = jnp.einsum(
            "td,tk->dk", normed_low, grad_projected, preferred_element_type=jnp.float32
        )
        grad_normed = jnp.einsum(
            "tk,dk->td", grad_projected, input_full, preferred_element_type=jnp.float32
        )
        grad_norm_one, gain_one_grad = norm_backward(grad_normed, gain_one, normed_first, inv_first)
        input_grads.append(grad_residual + grad_norm_one)
        reduced = (
            lax.psum_scatter(gain_one_grad, ("dp", "fsdp"), scatter_dimension=0, tiled=True),
            lax.psum_scatter(input_grad, ("dp", "fsdp"), scatter_dimension=0, tiled=True),
            lax.psum_scatter(kernel_grad, ("dp", "fsdp"), scatter_dimension=0, tiled=True),
            lax.psum_scatter(conv_bias_grad, ("dp", "fsdp"), scatter_dimension=0, tiled=True),
            lax.psum_scatter(select_grad, ("dp", "fsdp"), scatter_dimension=0, tiled=True),
            lax.psum_scatter(step_grad, ("dp", "fsdp"), scatter_dimension=0, tiled=True),
            lax.psum_scatter(step_bias_grad, ("dp", "fsdp"), scatter_dimension=0, tiled=True),
            lax.psum_scatter(decay_grad, ("dp", "fsdp"), scatter_dimension=0, tiled=True),
            lax.psum_scatter(skip_grad, ("dp", "fsdp"), scatter_dimension=0, tiled=True),
            lax.psum_scatter(output_grad, ("dp", "fsdp"), scatter_dimension=0, tiled=True),
            lax.psum_scatter(gain_two_grad, ("dp", "fsdp"), scatter_dimension=0, tiled=True),
            lax.psum_scatter(router_grad, ("dp", "fsdp"), scatter_dimension=0, tiled=True),
        )
        mamba_acc = tuple((total + piece for total, piece in zip(mamba_acc, reduced)))
    up_acc, down_acc = (
        lax.psum_scatter(up_acc.astype(jnp.bfloat16), "dp", scatter_dimension=2, tiled=True).astype(
            jnp.float32
        ),
        lax.psum_scatter(
            down_acc.astype(jnp.bfloat16), "dp", scatter_dimension=1, tiled=True
        ).astype(jnp.float32),
    )
    return (
        jnp.stack(outputs),
        jnp.stack(input_grads),
        mamba_acc[0],
        mamba_acc[1],
        mamba_acc[2],
        mamba_acc[3],
        mamba_acc[4],
        mamba_acc[5],
        mamba_acc[6],
        mamba_acc[7],
        mamba_acc[8],
        mamba_acc[9],
        mamba_acc[10],
        mamba_acc[11],
        up_acc,
        down_acc,
    )


def solution(mesh):
    placed = (
        P(None, ("dp", "fsdp"), None),
        P(None, ("dp", "fsdp"), None),
        P(None, ("dp", "fsdp"), None),
        P(None, ("dp", "fsdp"), None),
        P(("dp", "fsdp")),
        P(("dp", "fsdp"), None),
        P(("dp", "fsdp"), None),
        P(("dp", "fsdp")),
        P(("dp", "fsdp"), None),
        P(("dp", "fsdp"), None),
        P(("dp", "fsdp")),
        P(("dp", "fsdp"), None),
        P(("dp", "fsdp")),
        P(("dp", "fsdp"), None),
        P(("dp", "fsdp")),
        P(("dp", "fsdp"), None),
        P("fsdp", None, "dp"),
        P("fsdp", "dp", None),
    )
    return jax.shard_map(
        body,
        mesh=mesh,
        in_specs=placed,
        out_specs=(
            P(None, ("dp", "fsdp"), None),
            P(None, ("dp", "fsdp"), None),
            P(("dp", "fsdp")),
            P(("dp", "fsdp"), None),
            P(("dp", "fsdp"), None),
            P(("dp", "fsdp")),
            P(("dp", "fsdp"), None),
            P(("dp", "fsdp"), None),
            P(("dp", "fsdp")),
            P(("dp", "fsdp"), None),
            P(("dp", "fsdp")),
            P(("dp", "fsdp"), None),
            P(("dp", "fsdp")),
            P(("dp", "fsdp"), None),
            P("fsdp", None, "dp"),
            P("fsdp", "dp", None),
        ),
        check_vma=False,
    )
```

profile of v0, /device:TPU:8, one launch (start us, length us, event | category | flops | bytes accessed | tf_op | source)
XLA Modules:
  0.0 4549.1 jit_solution(8096141984638055651)
XLA Ops:
  55.0 61.0 %all-gather = bf16[32,48,4]{1,2,0:T(4,128)(2,1)S(1)} all-gather(bf16[1,48,4]{1,2,0:T(4,128)(2,1)S(1)} %bitcast.1909), channel_id=1, replica_groups=mesh['dp'=2,'fsdp'=16] {'dp','fsdp'}, dimensions={0}, use_global_device_ids=true | all-gather | bytes 12672 | tf_op jit(solution)/shard_map/all_gather | solution.py:128
  116.2 70.6 %all_gather.60 = bf16[1536,80]{1,0:T(8,128)(2,1)} all-gather(bf16[48,80]{1,0:T(8,128)(2,1)S(1)} %copy-done.107), channel_id=1, replica_groups=mesh['dp'=2,'fsdp'=16] {'dp','fsdp'}, dimensions={0}, use_global_device_ids=true | all-gather | bytes 253440 | tf_op jit(solution)/shard_map/all_gather | solution.py:130
  186.8 72.6 %all_gather.61 = bf16[1536,48]{1,0:T(8,128)(2,1)} all-gather(bf16[48,48]{1,0:T(8,128)(2,1)S(1)} %copy-done.108), channel_id=1, replica_groups=mesh['dp'=2,'fsdp'=16] {'dp','fsdp'}, dimensions={0}, use_global_device_ids=true | all-gather | bytes 152064 | tf_op jit(solution)/shard_map/all_gather | solution.py:131
  261.5 63.9 %all-gather.1 = bf16[32,48,16]{1,2,0:T(8,128)(2,1)S(1)} all-gather(bf16[1,48,16]{1,2,0:T(8,128)(2,1)S(1)} %bitcast.1907), channel_id=1, replica_groups=mesh['dp'=2,'fsdp'=16] {'dp','fsdp'}, dimensions={0}, use_global_device_ids=true | all-gather | bytes 50688 | tf_op jit(solution)/shard_map/all_gather | solution.py:133
  358.7 475.1 %while.341 = (s32[]{:T(128)}, f32[16,1536]{1,0:T(8,128)S(1)}, f32[8,32,1536]{2,1,0:T(8,128)}, f32[8,16,1536]{2,1,0:T(8,128)}, f32[8,32,1536]{2,1,0:T(8,128)}, /*...) while((s32[]{:T(128)}, f32[16,1536]{1,0:T(8,128)S(1)}, ...), condition=%wide.region_36.37_spmd, body=%wide.region_25.36_spmd.sunk | while | flops 1867787 | bytes 4194354 | solution.py:56
  363.2 52.6 %while.349 = (s32[]{:T(128)}, f32[16,1536]{1,0:T(8,128)S(1)}, f32[4,8,1536]{2,1,0:T(8,128)}, f32[4,8,1536]{2,1,0:T(8,128)}, f32[16,1536]{1,0:T(8,128)S(1)}, /*in...) while((s32[]{:T(128)}, f32[16,1536]{1,0:T(8,128)S(1)}, ...), condition=%wide.region_35.35_spmd, body=%wide.region_26.34_spmd.sunk | while | flops 1867785 | bytes 2414801 | solution.py:47
  839.0 473.1 %while.339 = (s32[]{:T(128)}, f32[16,1536]{1,0:T(8,128)S(1)}, f32[8,32,1536]{2,1,0:T(8,128)}, f32[8,16,1536]{2,1,0:T(8,128)}, f32[8,32,1536]{2,1,0:T(8,128)}, /*...) while((s32[]{:T(128)}, f32[16,1536]{1,0:T(8,128)S(1)}, ...), condition=%wide.region_14.15_spmd, body=%wide.region_3.14_spmd.sunk | while | flops 1867787 | bytes 4194354 | solution.py:56
  1335.1 67.5 %all-gather.2 = bf16[32,24,16]{1,2,0:T(8,128)(2,1)S(1)} all-gather(bf16[1,24,16]{1,2,0:T(8,128)(2,1)S(1)} %bitcast.1908), channel_id=1, replica_groups=mesh['dp'=2,'fsdp'=16] {'dp','fsdp'}, dimensions={0}, use_global_device_ids=true | all-gather | bytes 25344 | tf_op jit(solution)/shard_map/all_gather | solution.py:137
  1592.2 1050.7 %while.344 = (s32[]{:T(128)}, f32[16,1536]{1,0:T(8,128)S(1)}, f32[16,1536]{1,0:T(8,128)S(1)}, f32[8,32,1536]{2,1,0:T(8,128)}, f32[8,32,1536]{2,1,0:T(8,128)}, /*...) while((s32[]{:T(128)}, f32[16,1536]{1,0:T(8,128)S(1)}, ...), condition=%wide.region_83.84_spmd.clone, body=%wide.region_46.83_spmd.clone.sunk | while | flops 5173011 | bytes 24527320 | solution.py:56
  1649.5 72.6 %while.351 = (s32[]{:T(128)}, f32[16,1536]{1,0:T(8,128)S(1)}, f32[16,1536]{1,0:T(8,128)S(1)}, f32[4,8,1536]{2,1,0:T(8,128)S(1)}, f32[4,8,1536]{2,1,0:T(8,128)S(1...) while((s32[]{:T(128)}, f32[16,1536]{1,0:T(8,128)S(1)}, ...), condition=%wide.region_82.82_spmd.clone, body=%wide.region_49.81_spmd.clone.sunk | while | flops 3231499 | bytes 8916411 | solution.py:47
  1780.9 72.6 %while.351 = (s32[]{:T(128)}, f32[16,1536]{1,0:T(8,128)S(1)}, f32[16,1536]{1,0:T(8,128)S(1)}, f32[4,8,1536]{2,1,0:T(8,128)S(1)}, f32[4,8,1536]{2,1,0:T(8,128)S(1...) while((s32[]{:T(128)}, f32[16,1536]{1,0:T(8,128)S(1)}, ...), condition=%wide.region_82.82_spmd.clone, body=%wide.region_49.81_spmd.clone.sunk | while | flops 3231499 | bytes 8916411 | solution.py:47
  1912.2 72.6 %while.351 = (s32[]{:T(128)}, f32[16,1536]{1,0:T(8,128)S(1)}, f32[16,1536]{1,0:T(8,128)S(1)}, f32[4,8,1536]{2,1,0:T(8,128)S(1)}, f32[4,8,1536]{2,1,0:T(8,128)S(1...) while((s32[]{:T(128)}, f32[16,1536]{1,0:T(8,128)S(1)}, ...), condition=%wide.region_82.82_spmd.clone, body=%wide.region_49.81_spmd.clone.sunk | while | flops 3231499 | bytes 8916411 | solution.py:47
  2043.6 72.6 %while.351 = (s32[]{:T(128)}, f32[16,1536]{1,0:T(8,128)S(1)}, f32[16,1536]{1,0:T(8,128)S(1)}, f32[4,8,1536]{2,1,0:T(8,128)S(1)}, f32[4,8,1536]{2,1,0:T(8,128)S(1...) while((s32[]{:T(128)}, f32[16,1536]{1,0:T(8,128)S(1)}, ...), condition=%wide.region_82.82_spmd.clone, body=%wide.region_49.81_spmd.clone.sunk | while | flops 3231499 | bytes 8916411 | solution.py:47
  2174.9 72.6 %while.351 = (s32[]{:T(128)}, f32[16,1536]{1,0:T(8,128)S(1)}, f32[16,1536]{1,0:T(8,128)S(1)}, f32[4,8,1536]{2,1,0:T(8,128)S(1)}, f32[4,8,1536]{2,1,0:T(8,128)S(1...) while((s32[]{:T(128)}, f32[16,1536]{1,0:T(8,128)S(1)}, ...), condition=%wide.region_82.82_spmd.clone, body=%wide.region_49.81_spmd.clone.sunk | while | flops 3231499 | bytes 8916411 | solution.py:47
  2306.2 72.6 %while.351 = (s32[]{:T(128)}, f32[16,1536]{1,0:T(8,128)S(1)}, f32[16,1536]{1,0:T(8,128)S(1)}, f32[4,8,1536]{2,1,0:T(8,128)S(1)}, f32[4,8,1536]{2,1,0:T(8,128)S(1...) while((s32[]{:T(128)}, f32[16,1536]{1,0:T(8,128)S(1)}, ...), condition=%wide.region_82.82_spmd.clone, body=%wide.region_49.81_spmd.clone.sunk | while | flops 3231499 | bytes 8916411 | solution.py:47
  2437.6 72.6 %while.351 = (s32[]{:T(128)}, f32[16,1536]{1,0:T(8,128)S(1)}, f32[16,1536]{1,0:T(8,128)S(1)}, f32[4,8,1536]{2,1,0:T(8,128)S(1)}, f32[4,8,1536]{2,1,0:T(8,128)S(1...) while((s32[]{:T(128)}, f32[16,1536]{1,0:T(8,128)S(1)}, ...), condition=%wide.region_82.82_spmd.clone, body=%wide.region_49.81_spmd.clone.sunk | while | flops 3231499 | bytes 8916411 | solution.py:47
  2568.9 72.6 %while.351 = (s32[]{:T(128)}, f32[16,1536]{1,0:T(8,128)S(1)}, f32[16,1536]{1,0:T(8,128)S(1)}, f32[4,8,1536]{2,1,0:T(8,128)S(1)}, f32[4,8,1536]{2,1,0:T(8,128)S(1...) while((s32[]{:T(128)}, f32[16,1536]{1,0:T(8,128)S(1)}, ...), condition=%wide.region_82.82_spmd.clone, body=%wide.region_49.81_spmd.clone.sunk | while | flops 3231499 | bytes 8916411 | solution.py:47
  2652.8 1051.4 %while.347 = (s32[]{:T(128)}, f32[16,1536]{1,0:T(8,128)S(1)}, f32[16,1536]{1,0:T(8,128)S(1)}, f32[8,32,1536]{2,1,0:T(8,128)}, f32[8,32,1536]{2,1,0:T(8,128)}, /*...) while((s32[]{:T(128)}, f32[16,1536]{1,0:T(8,128)S(1)}, ...), condition=%wide.region_124.125_spmd.clone, body=%wide.region_87.124_spmd.clone.sunk | while | flops 5173011 | bytes 24527320 | solution.py:56
  2710.2 72.8 %while.353 = (s32[]{:T(128)}, f32[16,1536]{1,0:T(8,128)S(1)}, f32[16,1536]{1,0:T(8,128)S(1)}, f32[4,8,1536]{2,1,0:T(8,128)S(1)}, f32[4,8,1536]{2,1,0:T(8,128)S(1...) while((s32[]{:T(128)}, f32[16,1536]{1,0:T(8,128)S(1)}, ...), condition=%wide.region_123.123_spmd.clone, body=%wide.region_90.122_spmd.clone.sunk | while | flops 3231499 | bytes 8916411 | solution.py:47
  2841.6 72.8 %while.353 = (s32[]{:T(128)}, f32[16,1536]{1,0:T(8,128)S(1)}, f32[16,1536]{1,0:T(8,128)S(1)}, f32[4,8,1536]{2,1,0:T(8,128)S(1)}, f32[4,8,1536]{2,1,0:T(8,128)S(1...) while((s32[]{:T(128)}, f32[16,1536]{1,0:T(8,128)S(1)}, ...), condition=%wide.region_123.123_spmd.clone, body=%wide.region_90.122_spmd.clone.sunk | while | flops 3231499 | bytes 8916411 | solution.py:47
  2973.0 72.8 %while.353 = (s32[]{:T(128)}, f32[16,1536]{1,0:T(8,128)S(1)}, f32[16,1536]{1,0:T(8,128)S(1)}, f32[4,8,1536]{2,1,0:T(8,128)S(1)}, f32[4,8,1536]{2,1,0:T(8,128)S(1...) while((s32[]{:T(128)}, f32[16,1536]{1,0:T(8,128)S(1)}, ...), condition=%wide.region_123.123_spmd.clone, body=%wide.region_90.122_spmd.clone.sunk | while | flops 3231499 | bytes 8916411 | solution.py:47
  3104.4 72.8 %while.353 = (s32[]{:T(128)}, f32[16,1536]{1,0:T(8,128)S(1)}, f32[16,1536]{1,0:T(8,128)S(1)}, f32[4,8,1536]{2,1,0:T(8,128)S(1)}, f32[4,8,1536]{2,1,0:T(8,128)S(1...) while((s32[]{:T(128)}, f32[16,1536]{1,0:T(8,128)S(1)}, ...), condition=%wide.region_123.123_spmd.clone, body=%wide.region_90.122_spmd.clone.sunk | while | flops 3231499 | bytes 8916411 | solution.py:47
  3235.8 72.8 %while.353 = (s32[]{:T(128)}, f32[16,1536]{1,0:T(8,128)S(1)}, f32[16,1536]{1,0:T(8,128)S(1)}, f32[4,8,1536]{2,1,0:T(8,128)S(1)}, f32[4,8,1536]{2,1,0:T(8,128)S(1...) while((s32[]{:T(128)}, f32[16,1536]{1,0:T(8,128)S(1)}, ...), condition=%wide.region_123.123_spmd.clone, body=%wide.region_90.122_spmd.clone.sunk | while | flops 3231499 | bytes 8916411 | solution.py:47
  3367.3 72.8 %while.353 = (s32[]{:T(128)}, f32[16,1536]{1,0:T(8,128)S(1)}, f32[16,1536]{1,0:T(8,128)S(1)}, f32[4,8,1536]{2,1,0:T(8,128)S(1)}, f32[4,8,1536]{2,1,0:T(8,128)S(1...) while((s32[]{:T(128)}, f32[16,1536]{1,0:T(8,128)S(1)}, ...), condition=%wide.region_123.123_spmd.clone, body=%wide.region_90.122_spmd.clone.sunk | while | flops 3231499 | bytes 8916411 | solution.py:47
  3498.7 72.8 %while.353 = (s32[]{:T(128)}, f32[16,1536]{1,0:T(8,128)S(1)}, f32[16,1536]{1,0:T(8,128)S(1)}, f32[4,8,1536]{2,1,0:T(8,128)S(1)}, f32[4,8,1536]{2,1,0:T(8,128)S(1...) while((s32[]{:T(128)}, f32[16,1536]{1,0:T(8,128)S(1)}, ...), condition=%wide.region_123.123_spmd.clone, body=%wide.region_90.122_spmd.clone.sunk | while | flops 3231499 | bytes 8916411 | solution.py:47
  3630.1 72.8 %while.353 = (s32[]{:T(128)}, f32[16,1536]{1,0:T(8,128)S(1)}, f32[16,1536]{1,0:T(8,128)S(1)}, f32[4,8,1536]{2,1,0:T(8,128)S(1)}, f32[4,8,1536]{2,1,0:T(8,128)S(1...) while((s32[]{:T(128)}, f32[16,1536]{1,0:T(8,128)S(1)}, ...), condition=%wide.region_123.123_spmd.clone, body=%wide.region_90.122_spmd.clone.sunk | while | flops 3231499 | bytes 8916411 | solution.py:47
  3825.5 130.0 %all-reduce.39.cloned.1.call-done = (f32[768]{0:T(1024)}, f32[1536]{0:T(1024)}, f32[1536]{0:T(1024)}, f32[1536]{0:T(1024)}, f32[768]{0:T(1024)}, /*index=5*/f32[768,16]{0,1:T(8,128)}) async-done(((f32[768]{0:T(1024)}, f32[1536]{0:T(1024)}, f32[1536]{0:T(1024)}, f32[1536]{0:T(1024)}, f32[768]{0:T(1024)}, /*index=5*/f32[768,16]{0,1:T(8,128)}), (f32[768]{0:T(1024)}, f32[1536]{0:T(1024)}, f32[1536]{0:T(1024)}, ...) | async-done | bytes 73744
  3963.2 91.8 %reduce-scatter.28.cloned.1.call-done = f32[48,16]{1,0:T(8,128)} async-done(((f32[1536,16]{1,0:T(8,128)}), f32[48,16]{1,0:T(8,128)}) %reduce-scatter.28.cloned.1.call-update) | async-done | bytes 3088
  4091.2 97.3 %reduce-scatter.22.cloned.1.call-done = f32[48,48]{1,0:T(8,128)} async-done(((f32[1536,48]{1,0:T(8,128)}), f32[48,48]{1,0:T(8,128)}) %reduce-scatter.22.cloned.1.call-update) | async-done | bytes 9232 | tf_op jit(solution)/shard_map/reduce_scatter | solution.py:330
  4188.6 100.3 %reduce-scatter.20.cloned.1.call-done = f32[48,80]{1,0:T(8,128)} async-done(((f32[1536,80]{1,0:T(8,128)}), f32[48,80]{1,0:T(8,128)}) %reduce-scatter.20.cloned.1.call-update) | async-done | bytes 15376 | tf_op jit(solution)/shard_map/reduce_scatter | solution.py:329
  4288.8 112.0 %reduce-scatter.24.cloned.1.call-done = f32[48,768]{1,0:T(8,128)} async-done(((f32[1536,768]{1,0:T(8,128)}), f32[48,768]{1,0:T(8,128)}) %reduce-scatter.24.cloned.1.call-update) | async-done | bytes 147472 | tf_op jit(solution)/shard_map/reduce_scatter | solution.py:334
  4400.8 141.5 %reduce-scatter.18.cloned.1.call-done = f32[24,3072]{1,0:T(8,128)} async-done(((f32[768,3072]{1,0:T(8,128)}), f32[24,3072]{1,0:T(8,128)}) %reduce-scatter.18.cloned.1.call-update) | async-done | bytes 294928 | tf_op jit(solution)/shard_map/reduce_scatter | solution.py:326
  (8456 shorter events, 5094.7 us)
Async XLA Ops:
  7.2 320.4 %all-gather.8.cloned.1.call-start = ((), (), s32[]{:S(2)}) async-start(), calls=%async_computation.16 | async-start | bytes 4866048 | tf_op jit(solution)/shard_map/all_gather | solution.py:127
  7.9 1309.5 %all-gather.10.cloned.1.call-start = ((), (), s32[]{:S(2)}) async-start(), calls=%async_computation.17 | async-start | bytes 2433024 | tf_op jit(solution)/shard_map/all_gather | solution.py:135
  8.7 1405.8 %all-gather.12.cloned.1.call-start = ((), (), s32[]{:S(2)}) async-start(), calls=%async_computation.18 | async-start | bytes 7077888 | tf_op jit(solution)/shard_map/all_gather | solution.py:154
  9.5 1414.1 %all-gather.14.cloned.1.call-start = ((), (), s32[]{:S(2)}) async-start(), calls=%async_computation.19 | async-start | bytes 7077888 | tf_op jit(solution)/shard_map/all_gather | solution.py:155
  10.1 251.4 %copy-start.128 = (bf16[48,16]{0,1:T(8,128)(2,1)S(1)}, bf16[48,16]{0,1:T(8,128)(2,1)}, u32[]{:S(2)}) copy-start(bf16[48,16]{0,1:T(8,128)(2,1)} %param.49) | copy-start | bytes 4612
  10.4 251.0 %copy-start.90 = (s32[256]{0:T(256)}, s32[256]{0:T(256)S(1)}, u32[]{:S(2)}) copy-start(s32[256]{0:T(256)S(1)} %fusion.495) | copy-start | bytes 3076
  10.4 251.0 %copy-start.86 = (s32[1,256,1]{1,2,0:T(1,128)}, s32[1,256,1]{1,2,0:T(1,128)S(1)}, u32[]{:S(2)}) copy-start(s32[1,256,1]{1,2,0:T(1,128)S(1)} %get-tuple-element.3825) | copy-start | bytes 3076
  10.4 251.0 %copy-start.88 = (s32[1,256,1]{1,2,0:T(1,128)}, s32[1,256,1]{1,2,0:T(1,128)S(1)}, u32[]{:S(2)}) copy-start(s32[1,256,1]{1,2,0:T(1,128)S(1)} %get-tuple-element.3826) | copy-start | bytes 3076
  11.5 249.9 %copy-start.92 = (s32[256]{0:T(256)}, s32[256]{0:T(256)S(1)}, u32[]{:S(2)}) copy-start(s32[256]{0:T(256)S(1)} %fusion.496) | copy-start | bytes 3076
  54.8 277.2 %copy-start.63 = (f32[768]{0:T(1024)}, f32[768]{0:T(1024)S(1)}, u32[]{:S(2)}) copy-start(f32[768]{0:T(1024)S(1)} %convert_element_type.323) | copy-start | bytes 9220
  116.2 222.5 %copy-start.73 = (f32[1536]{0:T(1024)}, f32[1536]{0:T(1024)S(1)}, u32[]{:S(2)}) copy-start(f32[1536]{0:T(1024)S(1)} %get-tuple-element.3072) | copy-start | bytes 18436
  116.2 222.5 %copy-start.78 = (f32[1536]{0:T(1024)}, f32[1536]{0:T(1024)S(1)}, u32[]{:S(2)}) copy-start(f32[1536]{0:T(1024)S(1)} %get-tuple-element.3075) | copy-start | bytes 18436
  338.2 973.9 %copy-start = (f32[256,3072]{1,0:T(8,128)}, f32[256,3072]{1,0:T(8,128)S(1)}, u32[]{:S(2)}) copy-start(f32[256,3072]{1,0:T(8,128)S(1)} %fusion.482) | copy-start | bytes 9437188
  1324.7 79.4 %all-to-all-start.2 = ((bf16[16,20,768]{2,1,0:T(8,128)(2,1)}), bf16[16,20,768]{2,1,0:T(8,128)(2,1)S(1)}, u32[]{:S(2)}, u32[]{:S(2)}) async-start(bf16[16,20,768]{2,1,0:T(8,128)(2,1)} %reshape.3986), calls=%async_computation.2 | async-start | bytes 1179648 | tf_op jit(solution)/shard_map/all_to_all | solution.py:61
  1404.1 25.5 all-to-all-start
  1429.6 23.6 all-to-all-start.3
  1453.2 21.9 all-to-all-start.1
  1483.2 19.6 all-to-all-start.4
  1502.9 25.5 all-to-all-start.6
  1528.3 27.2 all-to-all-start.5
  1555.6 20.7 all-to-all-start.7
  1562.5 2261.6 %reduce-scatter.26.cloned.1.call-start = ((), (), s32[]{:S(2)}) async-start(), calls=%async_computation.26 | async-start | bytes 811008
  1592.2 1050.7 %copy-start.76 = (f32[1536]{0:T(1024)S(1)}, f32[1536]{0:T(1024)}, u32[]{:S(2)}) copy-start(f32[1536]{0:T(1024)} %convert_element_type.333) | copy-start | bytes 18436
  1592.2 1050.7 %copy-start.124 = (f32[256]{0:T(256)S(1)}, f32[256]{0:T(256)}, u32[]{:S(2)}) copy-start(f32[256]{0:T(256)} %get-tuple-element.3842) | copy-start | bytes 3076
  3730.1 225.3 %all-reduce.39.cloned.1.call-start = ((), (), s32[]{:S(2)}) async-start(), calls=%async_computation.28 | async-start | bytes 163840
  3743.5 311.4 %reduce-scatter.28.cloned.1.call-start = ((), (), s32[]{:S(2)}) async-start(), calls=%async_computation.27 | async-start | bytes 811008
  3744.8 325.1 %reduce-scatter.16.cloned.1.call-start = ((), (), s32[]{:S(2)}) async-start(), calls=%async_computation.21 | async-start | bytes 7077888 | tf_op jit(solution)/shard_map/reduce_scatter | solution.py:343
  3751.8 335.0 %reduce-scatter.14.cloned.1.call-start = ((), (), s32[]{:S(2)}) async-start(), calls=%async_computation.20 | async-start | bytes 7077888 | tf_op jit(solution)/shard_map/reduce_scatter | solution.py:340
  3761.7 426.9 %reduce-scatter.22.cloned.1.call-start = ((), (), s32[]{:S(2)}) async-start(), calls=%async_computation.24 | async-start | bytes 811008 | tf_op jit(solution)/shard_map/reduce_scatter | solution.py:330
  3764.5 524.3 %reduce-scatter.20.cloned.1.call-start = ((), (), s32[]{:S(2)}) async-start(), calls=%async_computation.23 | async-start | bytes 811008 | tf_op jit(solution)/shard_map/reduce_scatter | solution.py:329
  3769.3 631.5 %reduce-scatter.24.cloned.1.call-start = ((), (), s32[]{:S(2)}) async-start(), calls=%async_computation.25 | async-start | bytes 4866048 | tf_op jit(solution)/shard_map/reduce_scatter | solution.py:334
  3774.7 767.7 %reduce-scatter.18.cloned.1.call-start = ((), (), s32[]{:S(2)}) async-start(), calls=%async_computation.22 | async-start | bytes 9732096 | tf_op jit(solution)/shard_map/reduce_scatter | solution.py:326
  (131 other events, 2058.0 us)
Sparse Core Ops, SparseCore 0:
  10.9 65.4 all-gather.7
  79.3 55.1 all-gather.9
  136.0 14.5 all-gather.11
  152.0 15.6 all-gather.13
  3730.2 93.8 reduce-scatter.25
  3830.9 124.4 all-reduce.38
  3960.5 94.3 reduce-scatter.27
  4057.8 12.0 reduce-scatter.15
  4072.9 13.7 reduce-scatter.13
  4092.2 96.2 reduce-scatter.21
  4194.2 94.5 reduce-scatter.19
  4294.7 106.0 reduce-scatter.23
  4408.3 134.0 reduce-scatter.17
where the time goes:
time: 4610 us; the launch traced here: 4550 us
  other arithmetic  2210 us (48%)
  local copies, waits for them, and re-layouts  937 us (20%)
  waiting for transfers between devices  764 us (17%)
  blocking collectives  377 us (8%)
  matrix products  157 us (3%)
  starting transfers between devices  58.6 us (1%)
    reduce_sum x384, other arithmetic, one_step(): return (state, jnp.sum(cvec[:, None] * state, axis=0))  628 us
    reduce_sum x448, other arithmetic, one_step(): bvec[:, None] * (size_t * input_t)[None, :]  499 us
    reduce_sum x64, other arithmetic, one_step(): size_t[None, :] * decay_mat  445 us
    while x848, other arithmetic  414 us
    slice x448, local copies, waits for them, and re-layouts, block_step(): return lax.scan(one_step, state, block, unroll=8)  273 us
    unnamed x16, waiting for transfers between devices  262 us
    dynamic_update_slice x512, local copies, waits for them, and re-layouts, block_step(): return lax.scan(one_step, state, block, unroll=8)  210 us
    concatenate x192, other arithmetic, block_step(): return lax.scan(one_step, state, block, unroll=8)  155 us

commit v1 on v0

v1 whole, which is shorter than its diff:
```python
import functools
import math

import jax
import jax.numpy as jnp
from jax import lax
from jax.experimental import pallas as pl
from jax.experimental.pallas import tpu as pltpu
from jax.sharding import PartitionSpec as P

EPSILON = 1e-05
LOG2E = 1.4426950408889634
LN2 = 0.6931471805599453
LANES = 128
ROWS = 8


def fold_rows(parts):
    place = lax.broadcasted_iota(jnp.int32, parts[0].shape, 0)
    half = 1
    while half < ROWS:
        lower = (place & half) == 0
        merged = []
        for i in range(0, len(parts), 2):
            a, b = parts[i], parts[i + 1]
            merged.append(jnp.where(lower, a, b) + pltpu.roll(jnp.where(lower, b, a), half, 0))
        parts = merged
        half *= 2
    return parts[0]


def sum_states(parts, how, pick):
    if how == "mxu":
        stack = jnp.concatenate([p.astype(jnp.bfloat16) for p in parts], axis=0)
        return jnp.dot(pick, stack, preferred_element_type=jnp.float32)
    n = parts[0].shape[0]
    halves = []
    for p in parts:
        total = p[:ROWS]
        for i in range(1, n // ROWS):
            total = total + p[i * ROWS:(i + 1) * ROWS]
        halves.append(total)
    return fold_rows(halves)


def fwd_kernel(len_ref, delta_ref, xs_ref, b_ref, c_ref, a_ref, y_ref, h_ref, last_ref, state, *, block, how, group):
    pack, step = pl.program_id(0), pl.program_id(1)
    states, width = a_ref.shape

    @pl.when(step == 0)
    def _():
        state[...] = jnp.zeros_like(state)

    live = step * block < len_ref[pack]

    @pl.when(live)
    def _():
        pick = (lax.broadcasted_iota(jnp.int32, (ROWS, ROWS * states), 1) // states
                == lax.broadcasted_iota(jnp.int32, (ROWS, ROWS * states), 0)).astype(jnp.bfloat16)

        def rows(s, _):
            r = pl.multiple_of(s * ROWS, ROWS)

            def chunk(g, _):
                for u in range(group):
                    lanes = pl.ds(pl.multiple_of((g * group + u) * LANES, LANES), LANES)
                    d = delta_ref[pl.ds(r, ROWS), lanes]
                    dx = d * xs_ref[pl.ds(r, ROWS), lanes]
                    a = a_ref[:, lanes]
                    h = state[:, lanes]
                    parts = []
                    for t in range(ROWS):
                        h_ref[r + t, :, lanes] = h
                        e = jnp.exp2(d[t:t + 1] * a)
                        h = e * h + b_ref[r + t] * dx[t:t + 1]
                        parts.append(c_ref[r + t] * h)
                    state[:, lanes] = h
                    y_ref[pl.ds(r, ROWS), lanes] = sum_states(parts, how, pick)
                return 0

            lax.fori_loop(0, width // (LANES * group), chunk, 0)
            return 0

        lax.fori_loop(0, block // ROWS, rows, 0)

    @pl.when(jnp.logical_not(live))
    def _():
        y_ref[...] = jnp.zeros_like(y_ref)

    last_ref[0] = state[...]


def scan_fwd(lens, delta, xs, bwide, cwide, a2, steps, block=32, how="vpu", group=2):
    rows, width = delta.shape
    states = a2.shape[0]
    packs = rows // steps
    blocks = steps // block
    at = lambda p, i, lens: (p * blocks + i, 0)
    at3 = lambda p, i, lens: (p * blocks + i, 0, 0)
    return pl.pallas_call(
        functools.partial(fwd_kernel, block=block, how=how, group=group),
        grid_spec=pltpu.PrefetchScalarGridSpec(
            num_scalar_prefetch=1,
            grid=(packs, blocks),
            in_specs=[
                pl.BlockSpec((block, width), at),
                pl.BlockSpec((block, width), at),
                pl.BlockSpec((block, states, LANES), at3),
                pl.BlockSpec((block, states, LANES), at3),
                pl.BlockSpec((states, width), lambda p, i, lens: (0, 0)),
            ],
            out_specs=[
                pl.BlockSpec((block, width), at),
                pl.BlockSpec((block, states, width), at3),
                pl.BlockSpec((1, states, width), lambda p, i, lens: (p, 0, 0)),
            ],
            scratch_shapes=[pltpu.VMEM((states, width), jnp.float32)],
        ),
        out_shape=[
            jax.ShapeDtypeStruct((rows, width), jnp.float32),
            jax.ShapeDtypeStruct((rows, states, width), jnp.float32),
            jax.ShapeDtypeStruct((packs, states, width), jnp.float32),
        ],
        compiler_params=pltpu.CompilerParams(vmem_limit_bytes=48 << 20),
        name="scan_forward",
    )(lens, delta, xs, bwide, cwide, a2)


def bwd_kernel(len_ref, delta_ref, xs_ref, gy_ref, b_ref, c_ref, a_ref, h_ref, last_ref,
               gd_ref, gx_ref, gb_ref, gc_ref, ga_ref, mu_s, hn_s, *, block, how, group, blocks):
    pack, back = pl.program_id(0), pl.program_id(1)
    step = blocks - 1 - back
    states, width = a_ref.shape

    @pl.when(back == 0)
    def _():
        mu_s[...] = jnp.zeros_like(mu_s)
        hn_s[...] = last_ref[0]

    @pl.when((back == 0) & (pack == 0))
    def _():
        ga_ref[...] = jnp.zeros_like(ga_ref)

    live = step * block < len_ref[pack]

    gb_ref[...] = jnp.zeros_like(gb_ref)
    gc_ref[...] = jnp.zeros_like(gc_ref)

    @pl.when(live)
    def _():
        pick = (lax.broadcasted_iota(jnp.int32, (ROWS, ROWS * states), 1) // states
                == lax.broadcasted_iota(jnp.int32, (ROWS, ROWS * states), 0)).astype(jnp.bfloat16)

        def rows(s, _):
            r = pl.multiple_of((block // ROWS - 1 - s) * ROWS, ROWS)

            def chunk(g, _):
                each = []
                for u in range(group):
                    lanes = pl.ds(pl.multiple_of((g * group + u) * LANES, LANES), LANES)
                    d = delta_ref[pl.ds(r, ROWS), lanes]
                    x = xs_ref[pl.ds(r, ROWS), lanes]
                    gy = gy_ref[pl.ds(r, ROWS), lanes]
                    each.append(dict(lanes=lanes, d=d, x=x, gy=gy, dx=d * x, a=a_ref[:, lanes], mu=mu_s[:, lanes],
                                     hn=hn_s[:, lanes], ga=ga_ref[:, lanes], sp=[None] * ROWS, gp=[None] * ROWS))
                for t in range(ROWS - 1, -1, -1):
                    b, c = b_ref[r + t], c_ref[r + t]
                    gb = gc = None
                    for v in each:
                        dt = v["d"][t:t + 1]
                        gyt = v["gy"][t:t + 1]
                        hp = h_ref[r + t, :, v["lanes"]]
                        e = jnp.exp2(dt * v["a"])
                        lam = c * gyt + v["mu"]
                        v["sp"][t] = b * lam
                        one_b = lam * v["dx"][t:t + 1]
                        one_c = v["hn"] * gyt
                        gb = one_b if gb is None else gb + one_b
                        gc = one_c if gc is None else gc + one_c
                        mu = e * lam
                        q = mu * hp
                        v["gp"][t] = q * v["a"]
                        v["ga"] = v["ga"] + q * dt
                        v["mu"], v["hn"] = mu, hp
                    gb_ref[r + t] += gb
                    gc_ref[r + t] += gc
                for v in each:
                    lanes = v["lanes"]
                    mu_s[:, lanes], hn_s[:, lanes], ga_ref[:, lanes] = v["mu"], v["hn"], v["ga"]
                    total = sum_states(v["sp"], how, pick)
                    decay = sum_states(v["gp"], how, pick)
                    gd_ref[pl.ds(r, ROWS), lanes] = decay * LN2 + v["x"] * total
                    gx_ref[pl.ds(r, ROWS), lanes] = v["d"] * total
                return 0

            lax.fori_loop(0, width // (LANES * group), chunk, 0)
            return 0

        lax.fori_loop(0, block // ROWS, rows, 0)

    @pl.when(jnp.logical_not(live))
    def _():
        gd_ref[...] = jnp.zeros_like(gd_ref)
        gx_ref[...] = jnp.zeros_like(gx_ref)


def scan_bwd(lens, delta, xs, gy, bwide, cwide, a2, hall, last, steps, block=32, how="vpu", group=2):
    rows, width = delta.shape
    states = a2.shape[0]
    packs = rows // steps
    blocks = steps // block
    at = lambda p, i, lens: (p * blocks + blocks - 1 - i, 0)
    at3 = lambda p, i, lens: (p * blocks + blocks - 1 - i, 0, 0)
    f32 = jnp.float32
    return pl.pallas_call(
        functools.partial(bwd_kernel, block=block, how=how, group=group, blocks=blocks),
        grid_spec=pltpu.PrefetchScalarGridSpec(
            num_scalar_prefetch=1,
            grid=(packs, blocks),
            in_specs=[
                pl.BlockSpec((block, width), at),
                pl.BlockSpec((block, width), at),
                pl.BlockSpec((block, width), at),
                pl.BlockSpec((block, states, LANES), at3),
                pl.BlockSpec((block, states, LANES), at3),
                pl.BlockSpec((states, width), lambda p, i, lens: (0, 0)),
                pl.BlockSpec((block, states, width), at3),
                pl.BlockSpec((1, states, width), lambda p, i, lens: (p, 0, 0)),
            ],
            out_specs=[
                pl.BlockSpec((block, width), at),
                pl.BlockSpec((block, width), at),
                pl.BlockSpec((block, states, LANES), at3),
                pl.BlockSpec((block, states, LANES), at3),
                pl.BlockSpec((states, width), lambda p, i, lens: (0, 0)),
            ],
            scratch_shapes=[pltpu.VMEM((states, width), f32), pltpu.VMEM((states, width), f32)],
        ),
        out_shape=[
            jax.ShapeDtypeStruct((rows, width), f32),
            jax.ShapeDtypeStruct((rows, width), f32),
            jax.ShapeDtypeStruct((rows, states, LANES), f32),
            jax.ShapeDtypeStruct((rows, states, LANES), f32),
            jax.ShapeDtypeStruct((states, width), f32),
        ],
        compiler_params=pltpu.CompilerParams(vmem_limit_bytes=48 << 20),
        name="scan_backward",
    )(lens, delta, xs, gy, bwide, cwide, a2, hall, last)


F32 = jnp.float32
BF16 = jnp.bfloat16


def dot(left, right, dims=((1,), (0,))):
    return lax.dot_general(left, right, (dims, ((), ())), preferred_element_type=F32)


def swap(values, axis, mask):
    count = lax.axis_size(axis)
    return lax.ppermute(values, axis, [(i, i ^ mask) for i in range(count)])


def grow(values, axis, mask, dim):
    got = swap(values, axis, mask)
    upper = (lax.axis_index(axis) & mask) != 0
    return jnp.concatenate([jnp.where(upper, got, values), jnp.where(upper, values, got)], axis=dim)


def gather_rows(values):
    rows, width = values.shape
    bits = lax.axis_size("fsdp").bit_length() - 1
    whole = values.reshape((1,) * bits + (rows, width))
    place = lambda bit: bits - 1 - bit
    for bit in range(2, bits):
        whole = grow(whole, "fsdp", 1 << bit, place(bit))
    first, second = whole[..., : width // 2], whole[..., width // 2 :]
    first = grow(first, "fsdp", 2, place(1))
    second = grow(second, "fsdp", 1, place(0))
    first = grow(first, "fsdp", 1, place(0))
    second = grow(second, "fsdp", 2, place(1))
    whole = jnp.concatenate([first, second], axis=-1).reshape(-1, width)
    mask = 1
    while mask < lax.axis_size("dp"):
        whole = grow(whole, "dp", mask, 0) if mask == 1 else grow(whole.reshape(1, -1, width), "dp", mask, 0).reshape(-1, width)
        mask *= 2
    return whole


def own_block(values, index, count, axis):
    size = values.shape[axis] // count
    return lax.dynamic_slice_in_dim(values, index * size, size, axis)


def scatter_rows(piece):
    me, groups, count = lax.axis_index("dp"), lax.axis_size("dp"), lax.axis_size("fsdp")
    sent = [swap(piece(me ^ k).astype(BF16), "dp", k) for k in range(1, groups)]
    total = piece(me)
    for got in sent:
        total = total + got.astype(F32)
    rows, width = total.shape
    parts = total.astype(BF16).reshape(count, rows // count, width)
    return jnp.sum(lax.all_to_all(parts, "fsdp", 0, 0, tiled=True).astype(F32), axis=0)


def scatter_product(left, right):
    groups = lax.axis_size("dp")
    return scatter_rows(lambda i: dot(own_block(left, i, groups, 1), right, ((0,), (0,))))


def scatter_array(values):
    groups = lax.axis_size("dp")
    return scatter_rows(lambda i: own_block(values, i, groups, 0))


def norm_backward(grad_normed, gain, normed, inv_scale):
    scaled = grad_normed * gain
    grad_in = inv_scale * (scaled - normed * jnp.mean(scaled * normed, axis=-1, keepdims=True))
    return (grad_in, jnp.sum(grad_normed * normed, axis=0))


def shifted(values, by):
    if by == 0:
        return values
    zeros = jnp.zeros(values.shape[:1] + (abs(by),) + values.shape[2:], values.dtype)
    if by > 0:
        return jnp.concatenate([zeros, values[:, :-by]], axis=1)
    return jnp.concatenate([values[:, -by:], zeros], axis=1)


def body(
    tokens,
    cotangent,
    routes,
    lengths,
    norm1_gain,
    input_weight,
    conv_weight,
    conv_bias,
    scan_weight,
    step_weight,
    step_bias,
    decay_log,
    skip_gain,
    out_weight,
    norm2_gain,
    router_weight,
    expert_up,
    expert_down,
):
    micro, steps, model = tokens.shape
    rows = micro * steps
    experts = lax.axis_size("fsdp")
    groups = lax.axis_size("dp")
    devices = experts * groups
    capacity = (5 * steps + 4 * experts - 1) // (4 * experts)
    slots = micro * capacity
    inner = input_weight.shape[1] // 2
    states = decay_log.shape[1]
    rank = step_weight.shape[1]
    taps = conv_weight.shape[1]
    own_model, own_inner = norm1_gain.shape[0], conv_bias.shape[0]

    column = lambda v: v[:, None]
    half = experts // 2
    vectors = jnp.concatenate(
        [
            conv_weight,
            column(conv_bias),
            column(step_bias),
            column(skip_gain),
            decay_log,
            column(jnp.concatenate([norm1_gain, norm2_gain])),
            jnp.concatenate([router_weight[:, :half], router_weight[:, half:]], axis=0),
        ],
        axis=1,
    )
    used = vectors.shape[1]
    matrices = jnp.concatenate([scan_weight, step_weight], axis=1)
    small = jnp.concatenate(
        [matrices, vectors, jnp.zeros((own_inner, matrices.shape[1] - used), BF16)], axis=1
    )
    input_x = gather_rows(input_weight[:, :inner])
    small_full = gather_rows(small)
    input_z = lax.all_gather(input_weight[:, inner:], ("dp", "fsdp"), axis=0, tiled=True)
    output_full = lax.all_gather(out_weight, ("dp", "fsdp"), axis=0, tiled=True)
    ups = [expert_up[0]] + [swap(expert_up[0], "dp", k) for k in range(1, groups)]
    downs = [expert_down[0]] + [swap(expert_down[0], "dp", k) for k in range(1, groups)]

    place = jnp.arange(steps, dtype=jnp.int32)
    sample = lengths[:, 0, 0]
    live = (place[None, :] < sample[:, None]).astype(jnp.int32)
    route = routes[:, :, 0]
    expert_ids = jnp.arange(experts, dtype=jnp.int32)
    route_hot = (route[:, :, None] == expert_ids).astype(BF16)
    live_hot = route_hot * live[:, :, None].astype(BF16)
    earlier = (place[:, None] > place[None, :]).astype(BF16)
    before = lax.dot_general(
        jnp.broadcast_to(earlier, (micro, steps, steps)), live_hot, (((2,), (1,)), ((0,), (0,))),
        preferred_element_type=F32,
    )
    slot = jnp.sum(before * live_hot.astype(F32), axis=2).astype(jnp.int32)
    kept = (live * (slot < capacity).astype(jnp.int32)).reshape(rows)
    live = live.reshape(rows).astype(F32)
    target = (route * slots + jnp.arange(micro, dtype=jnp.int32)[:, None] * capacity + slot).reshape(rows)
    chooser = (
        (jnp.arange(experts * slots, dtype=jnp.int32)[:, None] == target[None, :]) & (kept[None, :] == 1)
    ).astype(BF16)
    kept = kept.astype(F32)
    route_float = route_hot.reshape(rows, experts).astype(F32)

    def to_experts(values):
        sent = dot(chooser, values).astype(BF16).reshape(experts, slots, -1)
        return lax.all_to_all(sent, "fsdp", 0, 0, tiled=True).reshape(experts * slots, -1)

    def from_experts(values):
        back = lax.all_to_all(values.reshape(experts, slots, -1), "fsdp", 0, 0, tiled=True)
        return dot(chooser, back.reshape(experts * slots, -1), ((0,), (0,)))

    cotangent = cotangent.reshape(rows, model)
    upstream_sent = to_experts(cotangent)
    upstream = cotangent.astype(F32)

    hidden = tokens.reshape(rows, model).astype(F32)
    matrices_full = small_full[:, : rank + 2 * states + rank]
    select_full = small_full[:, : rank + 2 * states]
    step_full = small_full[:, rank + 2 * states : 2 * rank + 2 * states]
    vectors_full = small_full[:, 2 * rank + 2 * states :].T
    kernel_full = vectors_full[:taps].astype(F32)
    bias_conv, bias_step, skip_one = [vectors_full[taps + i].astype(F32) for i in range(3)]
    decay_full = vectors_full[taps + 3 : taps + 3 + states].astype(F32)
    gains = vectors_full[taps + 3 + states].reshape(devices, 2, own_model)
    gain_one = gains[:, 0].reshape(model).astype(F32)
    gain_two = gains[:, 1].reshape(model).astype(F32)
    router_full = vectors_full[taps + 4 + states : taps + 4 + states + half].reshape(half, devices, 2, own_model)
    router_full = router_full.transpose(2, 0, 1, 3).reshape(experts, model)

    inv_first = lax.rsqrt(jnp.mean(hidden * hidden, axis=-1, keepdims=True) + EPSILON)
    normed_first = hidden * inv_first
    normed_low = (normed_first * gain_one).astype(BF16)
    branch_x = dot(normed_low, input_x)
    branch_x3 = branch_x.reshape(micro, steps, inner)
    conv_out = bias_conv
    for shift in range(taps):
        conv_out = conv_out + kernel_full[taps - 1 - shift] * shifted(branch_x3, shift)
    conv_out = conv_out.reshape(rows, inner)
    conv_sig = jax.nn.sigmoid(conv_out)
    scan_in = conv_out * conv_sig
    scan_low = scan_in.astype(BF16)
    selected = dot(scan_low, select_full)
    rank_low = selected[:, :rank].astype(BF16)
    bmat = selected[:, rank : rank + states]
    cmat = selected[:, rank + states :]
    step_pre = dot(rank_low, step_full, ((1,), (1,))) + bias_step
    step_size = jax.nn.softplus(step_pre)
    decay_mat = -jnp.exp(decay_full)
    decay_two = decay_mat * LOG2E
    bwide = jnp.broadcast_to(bmat[:, :, None], (rows, states, LANES))
    cwide = jnp.broadcast_to(cmat[:, :, None], (rows, states, LANES))
    scanned, state_all, state_last = scan_fwd(sample, step_size, scan_in, bwide, cwide, decay_two, steps, group=4)
    branch_z = dot(normed_low, input_z)
    mixer_out = scanned + skip_one * scan_in
    sigmoid_z = jax.nn.sigmoid(branch_z)
    silu_z = branch_z * sigmoid_z
    gated_low = (mixer_out * silu_z).astype(BF16)
    mixed = dot(gated_low, output_full)

    residual = hidden + live[:, None] * mixed
    inv_second = lax.rsqrt(jnp.mean(residual * residual, axis=-1, keepdims=True) + EPSILON)
    normed_second = residual * inv_second
    routed = (normed_second * gain_two).astype(BF16)
    probs = jax.nn.softmax(dot(routed, router_full, ((1,), (1,))), axis=-1)
    gate = jnp.sum(probs * route_float, axis=1)
    weight_row = gate * kept
    weight_high = weight_row.astype(BF16)
    weight_low = (weight_row - weight_high.astype(F32)).astype(BF16)
    received = to_experts(
        jnp.concatenate(
            [routed, weight_high[:, None], weight_low[:, None], jnp.zeros((rows, LANES - 2), BF16)], axis=1
        )
    )

    flat_in = received[:, :model]
    flat_weight = received[:, model].astype(F32) + received[:, model + 1].astype(F32)
    flat_grad = (flat_weight[:, None] * upstream_sent.astype(F32)).astype(BF16)
    pres = [dot(flat_in, up) for up in ups]
    acts = [jax.nn.gelu(pre).astype(BF16) for pre in pres]
    result = sum(dot(act, down) for act, down in zip(acts, downs))
    back = from_experts(result.astype(BF16))
    grad_pres = []
    for pre, down in zip(pres, downs):
        grad_act = dot(flat_grad, down, ((1,), (1,)))
        grad_pres.append(jax.vjp(jax.nn.gelu, pre)[1](grad_act)[0].astype(BF16))
    grad_rows = sum(dot(grad_pre, up, ((1,), (1,))) for grad_pre, up in zip(grad_pres, ups))
    grad_back = from_experts(grad_rows.astype(BF16))
    up_grad = dot(flat_in, grad_pres[0], ((0,), (0,)))
    down_grad = dot(acts[0], flat_grad, ((0,), (0,)))
    for k in range(1, groups):
        up_grad = up_grad + swap(dot(flat_in, grad_pres[k], ((0,), (0,))).astype(BF16), "dp", k).astype(F32)
        down_grad = down_grad + swap(dot(acts[k], flat_grad, ((0,), (0,))).astype(BF16), "dp", k).astype(F32)

    block_output = (residual + weight_row[:, None] * back).astype(BF16)
    grad_gate = kept * jnp.sum(upstream * back, axis=1)
    grad_logits = ((grad_gate * gate)[:, None] * (route_float - probs)).astype(BF16)
    router_grad = dot(routed, grad_logits, ((0,), (0,)))
    grad_routed = dot(grad_logits, router_full) + grad_back
    grad_norm_two, gain_two_grad = norm_backward(grad_routed, gain_two, normed_second, inv_second)
    grad_residual = upstream + grad_norm_two
    grad_mixed = (live[:, None] * grad_residual).astype(BF16)
    output_grad = scatter_product(gated_low, grad_mixed)

    grad_gated = dot(grad_mixed, output_full, ((1,), (1,)))
    grad_mixer = grad_gated * silu_z
    grad_z = (grad_gated * mixer_out * sigmoid_z * (1.0 + branch_z * (1.0 - sigmoid_z))).astype(BF16)
    input_z_grad = scatter_product(normed_low, grad_z)
    grad_step, grad_scan_in, grad_bwide, grad_cwide, grad_decay = scan_bwd(
        sample, step_size, scan_in, grad_mixer, bwide, cwide, decay_two, state_all, state_last, steps, group=4
    )
    skip_grad = jnp.sum(grad_mixer * scan_in, axis=0)
    decay_grad = grad_decay * decay_mat
    grad_step_pre = grad_step * jax.nn.sigmoid(step_pre)
    step_bias_grad = jnp.sum(grad_step_pre, axis=0)
    grad_step_low = grad_step_pre.astype(BF16)
    step_grad = dot(grad_step_low, rank_low, ((0,), (0,)))
    grad_rank = dot(grad_step_low, step_full)
    grad_selected = jnp.concatenate(
        [grad_rank, jnp.sum(grad_bwide, axis=-1), jnp.sum(grad_cwide, axis=-1)], axis=1
    ).astype(BF16)
    select_grad = dot(scan_low, grad_selected, ((0,), (0,)))
    grad_values = dot(grad_selected, select_full, ((1,), (1,)))
    grad_xs = grad_values + grad_scan_in + grad_mixer * skip_one
    grad_conv = grad_xs * (conv_sig * (1.0 + conv_out * (1.0 - conv_sig)))
    conv_bias_grad = jnp.sum(grad_conv, axis=0)
    grad_conv3 = grad_conv.reshape(micro, steps, inner)
    kernel_grad = []
    grad_x = 0.0
    for j in range(taps):
        shift = taps - 1 - j
        kernel_grad.append(jnp.sum(grad_conv3 * shifted(branch_x3, shift), axis=(0, 1)))
        grad_x = grad_x + kernel_full[j] * shifted(grad_conv3, -shift)
    grad_x = grad_x.reshape(rows, inner).astype(BF16)
    input_x_grad = scatter_product(normed_low, grad_x)
    grad_normed = dot(grad_x, input_x, ((1,), (1,))) + dot(grad_z, input_z, ((1,), (1,)))
    grad_norm_one, gain_one_grad = norm_backward(grad_normed, gain_one, normed_first, inv_first)
    tokens_grad = grad_residual + grad_norm_one

    gain_grads = jnp.concatenate(
        [gain_one_grad.reshape(devices, 1, own_model), gain_two_grad.reshape(devices, 1, own_model)], axis=1
    ).reshape(1, inner)
    router_grads = router_grad.reshape(devices, own_model, 2, half).transpose(0, 2, 1, 3).reshape(inner, half)
    vector_grads = jnp.concatenate(
        [jnp.stack(kernel_grad + [conv_bias_grad, step_bias_grad, skip_grad]), decay_grad, gain_grads], axis=0
    ).T
    small_grads = scatter_array(
        jnp.concatenate(
            [
                select_grad,
                step_grad,
                vector_grads,
                router_grads,
                jnp.zeros((inner, matrices.shape[1] - used), F32),
            ],
            axis=1,
        )
    )
    at = 2 * rank + 2 * states
    vector_grads = small_grads[:, at:]
    at_gain = taps + 3 + states
    routers = vector_grads[:, at_gain + 1 : at_gain + 1 + half]
    return (
        block_output.reshape(micro, steps, model),
        tokens_grad.reshape(micro, steps, model),
        vector_grads[:own_model, at_gain],
        jnp.concatenate([input_x_grad, input_z_grad], axis=1),
        vector_grads[:, :taps],
        vector_grads[:, taps],
        small_grads[:, : rank + 2 * states],
        small_grads[:, rank + 2 * states : at],
        vector_grads[:, taps + 1],
        vector_grads[:, taps + 3 : at_gain],
        vector_grads[:, taps + 2],
        output_grad,
        vector_grads[own_model:, at_gain],
        jnp.concatenate([routers[:own_model], routers[own_model:]], axis=1),
        up_grad[None],
        down_grad[None],
    )


def solution(mesh):
    rows3 = P(None, ("dp", "fsdp"), None)
    vector = P(("dp", "fsdp"))
    matrix = P(("dp", "fsdp"), None)
    weights = (
        vector, matrix, matrix, vector, matrix, matrix, vector, matrix, vector, matrix, vector, matrix,
        P("fsdp", None, "dp"), P("fsdp", "dp", None),
    )
    return jax.shard_map(
        body,
        mesh=mesh,
        in_specs=(rows3, rows3, rows3, rows3) + weights,
        out_specs=(rows3, rows3) + weights,
        check_vma=False,
    )
```

time: 4610 us -> 505 us (0.11); the launches traced: 4550 us -> 495 us
  other arithmetic: 2210 us -> 41.1 us
  local copies, waits for them, and re-layouts: 937 us -> 55.3 us
  waiting for transfers between devices: 764 us -> 121 us
  blocking collectives: 377 us -> 0 us
  Pallas kernels: 0 us -> 71.7 us
    reduce_sum x904 -> x8, other arithmetic: 1570 us -> 8.16 us  [the longest x1 3.38 us: body(): jnp.sum(grad_bwide, axis=-1)]
    reduce_scatter x6 -> x0, waiting for transfers between devices: 477 us -> none  [the longest x1 142 us: body(): lax.psum_scatter(input_grad, ('dp', 'fsdp'), scatter_dimension=0, tiled=T...]
    while x848 -> x0, other arithmetic: 414 us -> none
    all_gather x5 -> x0, blocking collectives: 336 us -> none  [the longest x1 72.6 us: body(): lax.all_gather(step_weight, ('dp', 'fsdp'), axis=0, tiled=True)]
    dynamic_update_slice x576 -> x0, local copies, waits for them, and re-layouts: 268 us -> none  [the longest x512 210 us: block_step(): return lax.scan(one_step, state, block, unroll=8)]
    unnamed x16 -> x2, waiting for transfers between devices: 262 us -> 0.03 us
    slice x457 -> x17, local copies, waits for them, and re-layouts: 274 us -> 15.7 us  [the longest x3 5.96 us: shifted(): return jnp.concatenate([values[:, -by:], zeros], axis=1)]
    concatenate x192 -> x15, other arithmetic: 155 us -> 1.92 us  [the longest x9 0.87 us: grow(): jnp.concatenate([jnp.where(upper, got, values), jnp.where(upper, values,...]
where the time goes in v1:
time: 505 us; the launch traced here: 495 us
  matrix products  127 us (25%)
  waiting for transfers between devices  121 us (24%)
  Pallas kernels  71.7 us (14%)
  starting transfers between devices  62 us (12%)
  local copies, waits for them, and re-layouts  55.3 us (11%)
  other arithmetic  41.1 us (8%)
  between operations  16.3 us (3%)
    dot_general x37, matrix products, dot(): lax.dot_general(left, right, (dims, ((), ())), preferred_element_type=F32)  127 us
    all_to_all x4, waiting for transfers between devices, scatter_rows(): lax.all_to_all(parts, 'fsdp', 0, 0, tiled=True).astype(F32)  43.6 us
    pallas_call x1, Pallas kernels, scan_bwd(): pl.pallas_call(functools.partial(bwd_kernel, block=block, how=how, group=...  42.8 us
    all_to_all x2, waiting for transfers between devices, to_experts(): lax.all_to_all(sent, 'fsdp', 0, 0, tiled=True).reshape(experts * slots, -1)  29.5 us
    pallas_call x1, Pallas kernels, scan_fwd(): pl.pallas_call(functools.partial(fwd_kernel, block=block, how=how, group=...  28.9 us
    all_to_all x4, starting transfers between devices, scatter_rows(): lax.all_to_all(parts, 'fsdp', 0, 0, tiled=True).astype(F32)  20.5 us
    unnamed x218, local copies, waits for them, and re-layouts  19.6 us
    ppermute x22, waiting for transfers between devices, swap(): return lax.ppermute(values, axis, [(i, i ^ mask) for i in range(count)])  17.6 us
  transfers between devices with their start and end apart: 32, of which 19 were waited for; matrix products, arithmetic and copies ran while one was open for 30% of the time, Pallas kernels for 6%

profile of v1, /device:TPU:8, one launch (start us, length us, event | category | flops | bytes accessed | tf_op | source)
XLA Modules:
  0.0 494.9 jit_solution(14043024202833753817)
XLA Ops:
  69.7 4.6 compare_select_fusion
  79.7 28.9 %scan_forward.1 = (f32[512,1536]{1,0:T(8,128)S(1)}, f32[512,16,1536]{2,1,0:T(8,128)}, f32[2,16,1536]{2,1,0:T(8,128)S(1)}) custom-call(s32[2]{0:T(128)S(1)} %slice_reduce_fusion.10.len_ref, f32[512,1536]{1,0:T(8,128)} %get-tuple-element.222.delta_ref, f32[512,1536]{1,0:T(8,128)} %copy-done.2, f32[512,16,128]{2,1,0:T(8,128)} %broadcast_in_dim.29.b_ref, ...), custom_call_target="tpu_custom_call" | custom-call | tf_op jit(solution)/shard_map/scan_forward/pallas_call | solution.py:100
  108.6 7.4 %multiply_convert_fusion.3 = (bf16[512,1536]{1,0:T(8,128)(2,1)}, f32[512,1536]{1,0:T(8,128)}) fusion(f32[512,1536]{1,0:T(8,128)S(1)} %get-tuple-element.24, f32[1536]{0:T(1024)S(1)} %get-tuple-element.152, f32[2,256,1536]{2,1,0:T(8,128)} %copy-done.10, bf16[512,768]{1,0:T(8,128)(2,1)} %fusion.30, bf16[768,1536]{1,0:T(8,128)(2,1)} %all-gather.3.cloned.1.call-done), kind=kOutput, calls=%fused_computation.45 | convolution fusion | flops 1217396736 | bytes 14161920 | tf_op jit(solution)/shard_map/dot_general | solution.py:256
  116.0 14.0 %all-gather.5.cloned.1.call-done = bf16[1536,768]{1,0:T(8,128)(2,1)} async-done(((bf16[48,768]{1,0:T(8,128)(2,1)}), bf16[1536,768]{1,0:T(8,128)(2,1)}) %all-gather.5.cloned.1.call-update) | async-done | bytes 2359312 | tf_op jit(solution)/shard_map/all_gather | solution.py:386
  141.5 6.0 %all-to-all-start = ((bf16[16,40,896]{2,1,0:T(8,128)(2,1)}), bf16[16,40,896]{2,1,0:T(8,128)(2,1)}, u32[]{:S(2)}, u32[]{:S(2)}) async-start(bf16[16,40,896]{2,1,0:T(8,128)(2,1)} %bitcast.209), calls=%async_computation | async-start | bytes 2293760 | tf_op jit(solution)/shard_map/all_to_all | solution.py:414
  150.8 24.8 %all-to-all-done = bf16[16,40,896]{2,1,0:T(8,128)(2,1)} async-done(((bf16[16,40,896]{2,1,0:T(8,128)(2,1)}), bf16[16,40,896]{2,1,0:T(8,128)(2,1)}, u32[]{:S(2)}, u32[]{:S(2)}) %all-to-all-start) | async-done | bytes 1146912 | tf_op jit(solution)/shard_map/all_to_all | solution.py:414
  175.7 5.7 %all-to-all-start.2 = ((bf16[16,40,768]{2,1,0:T(8,128)(2,1)}), bf16[16,40,768]{2,1,0:T(8,128)(2,1)}, u32[]{:S(2)}, u32[]{:S(2)}) async-start(bf16[16,40,768]{2,1,0:T(8,128)(2,1)} %bitcast.213), calls=%async_computation.2 | async-start | bytes 1966080 | tf_op jit(solution)/shard_map/all_to_all | solution.py:414
  181.4 5.6 %fusion.82 = f32[640,1536]{1,0:T(8,128)} fusion(bf16[640,896]{1,0:T(8,128)(2,1)} %bitcast.16, bf16[1,768,1536]{2,1,0:T(8,128)(2,1)} %param.34), kind=kOutput, calls=%fused_computation.145 | convolution fusion | flops 1509949440 | bytes 7274496 | tf_op jit(solution)/shard_map/dot_general | solution.py:256
  194.6 5.1 %add_convert_fusion.5 = bf16[640,768]{1,0:T(8,128)(2,1)} fusion(f32[640,768]{1,0:T(8,128)S(1)} %fusion.140, bf16[1536,768]{1,0:T(8,128)(2,1)} %collective-permute-done.15, f32[640,1536]{1,0:T(8,128)S(1)} %fusion.80), kind=kOutput, calls=%fused_computation.67 | convolution fusion | flops 1519779840 | bytes 9240576 | tf_op jit(solution)/shard_map/dot_general | solution.py:256
  199.7 4.7 all-to-all-done.2
  204.4 5.4 %all-to-all-start.1 = ((bf16[16,40,768]{2,1,0:T(8,128)(2,1)}), bf16[16,40,768]{2,1,0:T(8,128)(2,1)}, u32[]{:S(2)}, u32[]{:S(2)}) async-start(bf16[16,40,768]{2,1,0:T(8,128)(2,1)} %bitcast.212), calls=%async_computation.1 | async-start | bytes 1966080 | tf_op jit(solution)/shard_map/all_to_all | solution.py:417
  211.3 6.1 %fusion.6 = bf16[640,1536]{1,0:T(8,128)(2,1)S(1)} fusion(f32[640,1536]{1,0:T(8,128)} %fusion.82, bf16[640,768]{1,0:T(8,128)(2,1)S(1)} %bitcast.214, bf16[1,1536,768]{2,1,0:T(8,128)(2,1)} %param.35), kind=kOutput, calls=%fused_computation.13 | convolution fusion | flops 1529610240 | bytes 9240576 | tf_op jit(solution)/shard_map/dot_general | solution.py:256
  220.8 5.7 %fusion.13 = bf16[640,1536]{1,0:T(8,128)(2,1)S(1)} fusion(f32[640,1536]{1,0:T(8,128)S(1)} %copy-done.100, bf16[640,768]{1,0:T(8,128)(2,1)S(1)} %fusion.24, bf16[1536,768]{1,0:T(8,128)(2,1)} %collective-permute-done.15), kind=kOutput, calls=%fused_computation.20 | convolution fusion | flops 1529610240 | bytes 9240576 | tf_op jit(solution)/shard_map/dot_general | solution.py:256
  227.8 4.3 add_convert_fusion.4
  232.4 6.9 %all-to-all-start.3 = ((bf16[16,40,768]{2,1,0:T(8,128)(2,1)}), bf16[16,40,768]{2,1,0:T(8,128)(2,1)}, u32[]{:S(2)}, u32[]{:S(2)}) async-start(bf16[16,40,768]{2,1,0:T(8,128)(2,1)} %bitcast.211), calls=%async_computation.3 | async-start | bytes 1966080 | tf_op jit(solution)/shard_map/all_to_all | solution.py:417
  245.1 16.3 %all-to-all-done.3 = bf16[16,40,768]{2,1,0:T(8,128)(2,1)} async-done(((bf16[16,40,768]{2,1,0:T(8,128)(2,1)}), bf16[16,40,768]{2,1,0:T(8,128)(2,1)}, u32[]{:S(2)}, u32[]{:S(2)}) %all-to-all-start.3) | async-done | bytes 983072 | tf_op jit(solution)/shard_map/all_to_all | solution.py:417
  261.4 4.2 multiply_reduce_fusion.5
  268.3 8.1 %multiply_reduce_fusion = (f32[1536]{0:T(1024)}, f32[512,1536]{1,0:T(8,128)}, bf16[512,1536]{1,0:T(8,128)(2,1)}, f32[512,1536]{1,0:T(8,128)}) fusion(f32[2,256,1536]{2,1,0:T(8,128)S(1)} %copy-done.11, f32[512,1536]{1,0:T(8,128)} %get-tuple-element.225, f32[512,1536]{1,0:T(8,128)S(1)} %get-tuple-element.24, f32[1536]{0:T(1024)S(1)} %copy-done.68, ...), kind=kOutput, calls=%fused_computation.37 | convolution fusion | flops 1226832384 | bytes 20459520 | tf_op jit(solution)/shard_map/dot_general | solution.py:256
  276.4 42.8 %scan_backward.1 = (f32[512,1536]{1,0:T(8,128)S(1)}, f32[512,1536]{1,0:T(8,128)}, f32[512,16,128]{2,1,0:T(8,128)}, f32[512,16,128]{2,1,0:T(8,128)}, f32[16,1536]{1,0:T(8,128)S(1)}) custom-call(s32[2]{0:T(128)S(1)} %slice_reduce_fusion.10.len_ref, f32[512,1536]{1,0:T(8,128)} %get-tuple-element.222.delta_ref, f32[512,1536]{1,0:T(8,128)} %copy-done.2, ...), custom_call_target="tpu_custom_call" | custom-call | tf_op jit(solution)/shard_map/scan_backward/pallas_call | solution.py:215
  330.2 4.7 multiply_reduce_fusion.1
  346.9 5.5 %add_convert_fusion = bf16[2,256,1536]{2,1,0:T(8,128)(2,1)S(1)} fusion(f32[2,256,1536]{2,1,0:T(8,128)S(1)} %bitcast.197, f32[2,255,1536]{2,1,0:T(8,128)} %slice.244, f32[2,254,1536]{2,1,0:T(8,128)} %slice.243, f32[2,253,1536]{2,1,0:T(8,128)} %slice.242, f32[1536]{0:T(1024)S(1)} %copy-done.51, f32[1536]{0:T(1024)S(1)} %copy-done.53, f32[1536]{0:T(1024)S(1)} %copy-done.55, ...), kind=kLoop, calls=%fused_computation.43 | loop fusion | flops 6291456 | bytes 14106624 | tf_op jit(solution)/shard_map/convert_element_type | solution.py:541
  371.1 6.2 %all-to-all-start.4 = ((bf16[16,48,256]{2,1,0:T(8,128)(2,1)}), bf16[16,48,256]{2,1,0:T(8,128)(2,1)S(1)}, u32[]{:S(2)}, u32[]{:S(2)}) async-start(bf16[16,48,256]{2,1,0:T(8,128)(2,1)} %bitcast.34), calls=%async_computation.4 | async-start | bytes 786432 | tf_op jit(solution)/shard_map/all_to_all | solution.py:303
  380.8 8.5 %all-to-all-done.4 = bf16[16,48,256]{2,1,0:T(8,128)(2,1)S(1)} async-done(((bf16[16,48,256]{2,1,0:T(8,128)(2,1)}), bf16[16,48,256]{2,1,0:T(8,128)(2,1)S(1)}, u32[]{:S(2)}, u32[]{:S(2)}) %all-to-all-start.4) | async-done | bytes 393248 | tf_op jit(solution)/shard_map/all_to_all | solution.py:303
  390.0 4.8 all-to-all-start.6
  396.4 4.6 convolution_convert_fusion.1
  402.9 19.8 %all-to-all-done.6 = bf16[16,24,1536]{2,1,0:T(8,128)(2,1)S(1)} async-done(((bf16[16,24,1536]{2,1,0:T(8,128)(2,1)}), bf16[16,24,1536]{2,1,0:T(8,128)(2,1)S(1)}, u32[]{:S(2)}, u32[]{:S(2)}) %all-to-all-start.6) | async-done | bytes 1179680 | tf_op jit(solution)/shard_map/all_to_all | solution.py:303
  422.7 4.6 all-to-all-start.5
  427.3 6.3 %convolution_convert_fusion = bf16[1536,768]{1,0:T(8,128)(2,1)} fusion(bf16[640,768]{1,0:T(8,128)(2,1)S(1)} %copy-done.36, f32[640,1536]{1,0:T(8,128)} %copy-done.99), kind=kOutput, calls=%fused_computation.23 | convolution fusion | flops 1519976448 | bytes 7274496 | tf_op jit(solution)/shard_map/dot_general | solution.py:256
  441.8 12.7 %all-to-all-done.5 = bf16[16,24,1536]{2,1,0:T(8,128)(2,1)S(1)} async-done(((bf16[16,24,1536]{2,1,0:T(8,128)(2,1)}), bf16[16,24,1536]{2,1,0:T(8,128)(2,1)S(1)}, u32[]{:S(2)}, u32[]{:S(2)}) %all-to-all-start.5) | async-done | bytes 1179680 | tf_op jit(solution)/shard_map/all_to_all | solution.py:303
  454.6 4.9 all-to-all-start.7
  459.5 6.9 %add_bitcast_fusion.1 = f32[1,768,1536]{2,1,0:T(8,128)} fusion(bf16[768,1536]{1,0:T(8,128)(2,1)} %collective-permute-done.20, bf16[640,1536]{1,0:T(8,128)(2,1)} %copy-done.96, bf16[640,896]{1,0:T(8,128)(2,1)} %bitcast.16), kind=kOutput, calls=%fused_computation.6 | convolution fusion | flops 1512308736 | bytes 10027008 | tf_op jit(solution)/shard_map/dot_general | solution.py:256
  466.5 6.5 %add_bitcast_fusion = f32[1,1536,768]{2,1,0:T(8,128)} fusion(bf16[1536,768]{1,0:T(8,128)(2,1)} %collective-permute-done.21, bf16[640,768]{1,0:T(8,128)(2,1)S(1)} %copy-done.37, f32[640,1536]{1,0:T(8,128)S(1)} %copy-done.98), kind=kOutput, calls=%fused_computation.5 | convolution fusion | flops 1521156096 | bytes 11993088 | tf_op jit(solution)/shard_map/dot_general | solution.py:256
  (424 shorter events, 175.9 us)
Async XLA Ops:
  7.2 101.4 %all-gather.3.cloned.1.call-start = ((), (), s32[]{:S(2)}) async-start(), calls=%async_computation.8 | async-start | bytes 2433024 | tf_op jit(solution)/shard_map/all_gather | solution.py:385
  8.9 121.2 %all-gather.5.cloned.1.call-start = ((), (), s32[]{:S(2)}) async-start(), calls=%async_computation.9 | async-start | bytes 2433024 | tf_op jit(solution)/shard_map/all_gather | solution.py:386
  15.3 7.3 %collective-permute-start = (bf16[1,1,1,1,48,256]{5,4,3,2,1,0:T(8,128)(2,1)S(1)}, bf16[1,1,1,1,48,256]{5,4,3,2,1,0:T(8,128)(2,1)S(1)}, u32[]{:S(2)}, u32[]{:S(2)}) collective-permute-start(bf16[1,1,1,1,48,256]{5,4,3,2,1,0:T(8,128)(2,1)S(1)} %bitcast.218), channel_id=1, source_target_pairs={{0,4},{1,5},{2,6},{3,7},{4,0},{5,1},{6,2},{7,3},{8,12},{9,13},{10,... | collective-permute-start | bytes 73736 | tf_op jit(solution)/shard_map/ppermute | solution.py:261
  15.4 15.6 %collective-permute-start.7 = (bf16[1,1,1,1,24,1536]{5,4,3,2,1,0:T(8,128)(2,1)S(1)}, bf16[1,1,1,1,24,1536]{5,4,3,2,1,0:T(8,128)(2,1)S(1)}, u32[]{:S(2)}, u32[]{:S(2)}) collective-permute-start(bf16[1,1,1,1,24,1536]{5,4,3,2,1,0:T(8,128)(2,1)S(1)} %get-tuple-element.199), channel_id=1, source_target_pairs={{0,4},{1,5},{2,6},{3,7},{4,0},{5,1},{6,2},{7,3},{8,12},{9,13},{10,... | collective-permute-start | bytes 221192 | tf_op jit(solution)/shard_map/ppermute | solution.py:261
  22.6 5.1 %collective-permute-start.1 = (bf16[1,2,1,1,48,256]{5,4,3,2,1,0:T(8,128)(2,1)S(1)}, bf16[1,2,1,1,48,256]{5,4,3,2,1,0:T(8,128)(2,1)S(1)}, u32[]{:S(2)}, u32[]{:S(2)}) collective-permute-start(bf16[1,2,1,1,48,256]{5,4,3,2,1,0:T(8,128)(2,1)S(1)} %pad_maximum_fusion.15), channel_id=1, source_target_pairs={{0,8},{1,9},{2,10},{3,11},{4,12},{5,13},{6,14},{7,15},{8,0},{9,1},... | collective-permute-start | bytes 147464 | tf_op jit(solution)/shard_map/ppermute | solution.py:261
  27.8 6.4 %collective-permute-start.4 = (bf16[2,2,1,1,48,128]{5,4,3,2,1,0:T(8,128)(2,1)S(1)}, bf16[2,2,1,1,48,128]{5,4,3,2,1,0:T(8,128)(2,1)S(1)}, u32[]{:S(2)}, u32[]{:S(2)}) collective-permute-start(bf16[2,2,1,1,48,128]{5,4,3,2,1,0:T(8,128)(2,1)S(1)} %get-tuple-element.203), channel_id=1, source_target_pairs={{0,1},{1,0},{2,3},{3,2},{4,5},{5,4},{6,7},{7,6},{8,9},{9,8},{10,11... | collective-permute-start | bytes 147464 | tf_op jit(solution)/shard_map/ppermute | solution.py:261
  29.4 5.4 %collective-permute-start.2 = (bf16[2,2,1,1,48,128]{5,4,3,2,1,0:T(8,128)(2,1)S(1)}, bf16[2,2,1,1,48,128]{5,4,3,2,1,0:T(8,128)(2,1)S(1)}, u32[]{:S(2)}, u32[]{:S(2)}) collective-permute-start(bf16[2,2,1,1,48,128]{5,4,3,2,1,0:T(8,128)(2,1)S(1)} %get-tuple-element.202), channel_id=1, source_target_pairs={{0,2},{1,3},{2,0},{3,1},{4,6},{5,7},{6,4},{7,5},{8,10},{9,11},{10,... | collective-permute-start | bytes 147464 | tf_op jit(solution)/shard_map/ppermute | solution.py:261
  31.1 6.7 %collective-permute-start.8 = (bf16[1,2,1,1,24,1536]{5,4,3,2,1,0:T(8,128)(2,1)S(1)}, bf16[1,2,1,1,24,1536]{5,4,3,2,1,0:T(8,128)(2,1)S(1)}, u32[]{:S(2)}, u32[]{:S(2)}) collective-permute-start(bf16[1,2,1,1,24,1536]{5,4,3,2,1,0:T(8,128)(2,1)S(1)} %pad_maximum_fusion.10), channel_id=1, source_target_pairs={{0,8},{1,9},{2,10},{3,11},{4,12},{5,13},{6,14},{7,15},{8,0},{9,1},... | collective-permute-start | bytes 442376 | tf_op jit(solution)/shard_map/ppermute | solution.py:261
  34.3 4.7 collective-permute-start.5
  34.8 5.0 %collective-permute-start.3 = (bf16[2,2,2,1,48,128]{5,4,3,2,1,0:T(8,128)(2,1)S(1)}, bf16[2,2,2,1,48,128]{5,4,3,2,1,0:T(8,128)(2,1)S(1)}, u32[]{:S(2)}, u32[]{:S(2)}) collective-permute-start(bf16[2,2,2,1,48,128]{5,4,3,2,1,0:T(8,128)(2,1)S(1)} %pad_maximum_fusion.11), channel_id=1, source_target_pairs={{0,1},{1,0},{2,3},{3,2},{4,5},{5,4},{6,7},{7,6},{8,9},{9,8},{10,11... | collective-permute-start | bytes 294920 | tf_op jit(solution)/shard_map/ppermute | solution.py:261
  37.8 6.9 %collective-permute-start.11 = (bf16[2,2,1,1,24,768]{5,4,3,2,1,0:T(8,128)(2,1)S(1)}, bf16[2,2,1,1,24,768]{5,4,3,2,1,0:T(8,128)(2,1)S(1)}, u32[]{:S(2)}, u32[]{:S(2)}) collective-permute-start(bf16[2,2,1,1,24,768]{5,4,3,2,1,0:T(8,128)(2,1)S(1)} %get-tuple-element.185), channel_id=1, source_target_pairs={{0,1},{1,0},{2,3},{3,2},{4,5},{5,4},{6,7},{7,6},{8,9},{9,8},{10,11... | collective-permute-start | bytes 442376 | tf_op jit(solution)/shard_map/ppermute | solution.py:261
  40.1 8.3 %collective-permute-start.6 = (bf16[768,256]{0,1:T(8,128)(2,1)S(1)}, bf16[768,256]{0,1:T(8,128)(2,1)S(1)}, u32[]{:S(2)}, u32[]{:S(2)}) collective-permute-start(bf16[768,256]{0,1:T(8,128)(2,1)S(1)} %copy.176), channel_id=1, source_target_pairs={{0,16},{16,0},{1,17},{17,1},{2,18},{18,2},{3,19},{19,3},{4,20},{20... | collective-permute-start | bytes 1179656 | tf_op jit(solution)/shard_map/ppermute | solution.py:261
  40.1 6.7 %collective-permute-start.9 = (bf16[2,2,1,1,24,768]{5,4,3,2,1,0:T(8,128)(2,1)S(1)}, bf16[2,2,1,1,24,768]{5,4,3,2,1,0:T(8,128)(2,1)S(1)}, u32[]{:S(2)}, u32[]{:S(2)}) collective-permute-start(bf16[2,2,1,1,24,768]{5,4,3,2,1,0:T(8,128)(2,1)S(1)} %get-tuple-element.184), channel_id=1, source_target_pairs={{0,2},{1,3},{2,0},{3,1},{4,6},{5,7},{6,4},{7,5},{8,10},{9,11},{10,... | collective-permute-start | bytes 442376 | tf_op jit(solution)/shard_map/ppermute | solution.py:261
  44.8 8.0 %collective-permute-start.12 = (bf16[2,2,1,2,24,768]{5,4,3,2,1,0:T(8,128)(2,1)S(1)}, bf16[2,2,1,2,24,768]{5,4,3,2,1,0:T(8,128)(2,1)}, u32[]{:S(2)}, u32[]{:S(2)}) collective-permute-start(bf16[2,2,1,2,24,768]{5,4,3,2,1,0:T(8,128)(2,1)S(1)} %pad_maximum_fusion.6), channel_id=1, source_target_pairs={{0,2},{1,3},{2,0},{3,1},{4,6},{5,7},{6,4},{7,5},{8,10},{9,11},{10,... | collective-permute-start | bytes 884744 | tf_op jit(solution)/shard_map/ppermute | solution.py:261
  47.6 8.5 %collective-permute-start.10 = (bf16[2,2,2,1,24,768]{5,4,3,2,1,0:T(8,128)(2,1)}, bf16[2,2,2,1,24,768]{5,4,3,2,1,0:T(8,128)(2,1)}, u32[]{:S(2)}, u32[]{:S(2)}) collective-permute-start(bf16[2,2,2,1,24,768]{5,4,3,2,1,0:T(8,128)(2,1)} %pad_maximum_fusion.5), channel_id=1, source_target_pairs={{0,1},{1,0},{2,3},{3,2},{4,5},{5,4},{6,7},{7,6},{8,9},{9,8},{10,11... | collective-permute-start | bytes 884744 | tf_op jit(solution)/shard_map/ppermute | solution.py:261
  57.4 3.0 collective-permute-start.13
  141.5 34.2 %all-to-all-start = ((bf16[16,40,896]{2,1,0:T(8,128)(2,1)}), bf16[16,40,896]{2,1,0:T(8,128)(2,1)}, u32[]{:S(2)}, u32[]{:S(2)}) async-start(bf16[16,40,896]{2,1,0:T(8,128)(2,1)} %bitcast.209), calls=%async_computation | async-start | bytes 2293760 | tf_op jit(solution)/shard_map/all_to_all | solution.py:414
  147.5 40.8 %collective-permute-start.14 = (bf16[768,1536]{1,0:T(8,128)(2,1)}, bf16[768,1536]{1,0:T(8,128)(2,1)}, u32[]{:S(2)}, u32[]{:S(2)}) collective-permute-start(bf16[768,1536]{1,0:T(8,128)(2,1)} %bitcast.240), channel_id=1, source_target_pairs={{0,16},{16,0},{1,17},{17,1},{2,18},{18,2},{3,19},{19,3},{4,20},{20... | collective-permute-start | bytes 7077896 | tf_op jit(solution)/shard_map/ppermute | solution.py:261
  147.5 47.1 %collective-permute-start.15 = (bf16[1536,768]{1,0:T(8,128)(2,1)}, bf16[1536,768]{1,0:T(8,128)(2,1)}, u32[]{:S(2)}, u32[]{:S(2)}) collective-permute-start(bf16[1536,768]{1,0:T(8,128)(2,1)} %bitcast.239), channel_id=1, source_target_pairs={{0,16},{16,0},{1,17},{17,1},{2,18},{18,2},{3,19},{19,3},{4,20},{20... | collective-permute-start | bytes 7077896 | tf_op jit(solution)/shard_map/ppermute | solution.py:261
  175.7 28.7 %all-to-all-start.2 = ((bf16[16,40,768]{2,1,0:T(8,128)(2,1)}), bf16[16,40,768]{2,1,0:T(8,128)(2,1)}, u32[]{:S(2)}, u32[]{:S(2)}) async-start(bf16[16,40,768]{2,1,0:T(8,128)(2,1)} %bitcast.213), calls=%async_computation.2 | async-start | bytes 1966080 | tf_op jit(solution)/shard_map/all_to_all | solution.py:414
  204.4 28.1 %all-to-all-start.1 = ((bf16[16,40,768]{2,1,0:T(8,128)(2,1)}), bf16[16,40,768]{2,1,0:T(8,128)(2,1)}, u32[]{:S(2)}, u32[]{:S(2)}) async-start(bf16[16,40,768]{2,1,0:T(8,128)(2,1)} %bitcast.212), calls=%async_computation.1 | async-start | bytes 1966080 | tf_op jit(solution)/shard_map/all_to_all | solution.py:417
  232.4 28.9 %all-to-all-start.3 = ((bf16[16,40,768]{2,1,0:T(8,128)(2,1)}), bf16[16,40,768]{2,1,0:T(8,128)(2,1)}, u32[]{:S(2)}, u32[]{:S(2)}) async-start(bf16[16,40,768]{2,1,0:T(8,128)(2,1)} %bitcast.211), calls=%async_computation.3 | async-start | bytes 1966080 | tf_op jit(solution)/shard_map/all_to_all | solution.py:417
  361.7 15.6 %collective-permute-start.18 = (bf16[384,1536]{1,0:T(8,128)(2,1)}, bf16[384,1536]{1,0:T(8,128)(2,1)}, u32[]{:S(2)}, u32[]{:S(2)}) collective-permute-start(bf16[384,1536]{1,0:T(8,128)(2,1)} %convolution_convert_fusion.2), channel_id=1, source_target_pairs={{0,16},{16,0},{1,17},{17,1},{2,18},{18,2},{3,19},{19,3},{4,20},{20... | collective-permute-start | bytes 3538952 | tf_op jit(solution)/shard_map/ppermute | solution.py:261
  368.5 1.8 collective-permute-start.16
  371.1 18.2 %all-to-all-start.4 = ((bf16[16,48,256]{2,1,0:T(8,128)(2,1)}), bf16[16,48,256]{2,1,0:T(8,128)(2,1)S(1)}, u32[]{:S(2)}, u32[]{:S(2)}) async-start(bf16[16,48,256]{2,1,0:T(8,128)(2,1)} %bitcast.34), calls=%async_computation.4 | async-start | bytes 786432 | tf_op jit(solution)/shard_map/all_to_all | solution.py:303
  390.0 32.7 %all-to-all-start.6 = ((bf16[16,24,1536]{2,1,0:T(8,128)(2,1)}), bf16[16,24,1536]{2,1,0:T(8,128)(2,1)S(1)}, u32[]{:S(2)}, u32[]{:S(2)}) async-start(bf16[16,24,1536]{2,1,0:T(8,128)(2,1)} %bitcast.208), calls=%async_computation.6 | async-start | bytes 2359296 | tf_op jit(solution)/shard_map/all_to_all | solution.py:303
  395.7 5.4 %collective-permute-start.17 = (bf16[384,1536]{1,0:T(8,128)(2,1)S(1)}, bf16[384,1536]{1,0:T(8,128)(2,1)S(1)}, u32[]{:S(2)}, u32[]{:S(2)}) collective-permute-start(bf16[384,1536]{1,0:T(8,128)(2,1)S(1)} %convolution_convert_fusion.3), channel_id=1, source_target_pairs={{0,16},{16,0},{1,17},{17,1},{2,18},{18,2},{3,19},{19,3},{4,20},{20... | collective-permute-start | bytes 3538952 | tf_op jit(solution)/shard_map/ppermute | solution.py:261
  401.1 58.5 %collective-permute-start.20 = (bf16[768,1536]{1,0:T(8,128)(2,1)}, bf16[768,1536]{1,0:T(8,128)(2,1)}, u32[]{:S(2)}, u32[]{:S(2)}) collective-permute-start(bf16[768,1536]{1,0:T(8,128)(2,1)} %convolution_convert_fusion.1), channel_id=1, source_target_pairs={{0,16},{16,0},{1,17},{17,1},{2,18},{18,2},{3,19},{19,3},{4,20},{20... | collective-permute-start | bytes 7077896 | tf_op jit(solution)/shard_map/ppermute | solution.py:261
  422.7 31.9 %all-to-all-start.5 = ((bf16[16,24,1536]{2,1,0:T(8,128)(2,1)}), bf16[16,24,1536]{2,1,0:T(8,128)(2,1)S(1)}, u32[]{:S(2)}, u32[]{:S(2)}) async-start(bf16[16,24,1536]{2,1,0:T(8,128)(2,1)} %bitcast.207), calls=%async_computation.5 | async-start | bytes 2359296 | tf_op jit(solution)/shard_map/all_to_all | solution.py:303
  433.7 32.8 %collective-permute-start.21 = (bf16[1536,768]{1,0:T(8,128)(2,1)}, bf16[1536,768]{1,0:T(8,128)(2,1)}, u32[]{:S(2)}, u32[]{:S(2)}) collective-permute-start(bf16[1536,768]{1,0:T(8,128)(2,1)} %convolution_convert_fusion), channel_id=1, source_target_pairs={{0,16},{16,0},{1,17},{17,1},{2,18},{18,2},{3,19},{19,3},{4,20},{20... | collective-permute-start | bytes 7077896 | tf_op jit(solution)/shard_map/ppermute | solution.py:261
  434.6 5.4 %collective-permute-start.19 = (bf16[768,768]{1,0:T(8,128)(2,1)S(1)}, bf16[768,768]{1,0:T(8,128)(2,1)S(1)}, u32[]{:S(2)}, u32[]{:S(2)}) collective-permute-start(bf16[768,768]{1,0:T(8,128)(2,1)S(1)} %convolution_convert_fusion.4), channel_id=1, source_target_pairs={{0,16},{16,0},{1,17},{17,1},{2,18},{18,2},{3,19},{19,3},{4,20},{20... | collective-permute-start | bytes 3538952 | tf_op jit(solution)/shard_map/ppermute | solution.py:261
  454.6 32.1 %all-to-all-start.7 = ((bf16[16,48,768]{2,1,0:T(8,128)(2,1)}), bf16[16,48,768]{2,1,0:T(8,128)(2,1)S(1)}, u32[]{:S(2)}, u32[]{:S(2)}) async-start(bf16[16,48,768]{2,1,0:T(8,128)(2,1)} %bitcast.206), calls=%async_computation.7 | async-start | bytes 2359296 | tf_op jit(solution)/shard_map/all_to_all | solution.py:303
  (103 other events, 1041.2 us)
Sparse Core Ops, SparseCore 0:
  11.5 59.4 all-gather.2
  73.9 56.1 all-gather.4
